TPU v7x, 32 devices: a whole 2x2x4 slice. The times are simulated.
32 devices in a mesh: pipe: 2 (over core), dp: 8 (over z, x), tensor: 2 (over y).
Axes of the slice: x: 2, y: 2, z: 4, core: 2. Of those that a mesh axis runs over, the one named last changes fastest.
Arguments:
- block_input: bfloat16 [2, 1024, 2048], P(None, ('dp', 'tensor')), may hold values from -6 to 6
- cotangent: bfloat16 [2, 1024, 2048], P(None, ('dp', 'tensor')), may hold values from -6 to 6
- segments: int32 [2, 1024], replicated, may hold values from 0 to 3, never falling along the last dimension, each value on 1 to 512 neighbouring positions
- norm_gains: float32 [2, 2, 2048], P('pipe', None, ('dp', 'tensor')), may hold values from 0.5 to 1.5
- w_query: bfloat16 [2, 2048, 2048], P('pipe', 'dp', 'tensor'), may hold values from -0.125 to 0.125
- key_matrix: bfloat16 [2, 2048, 512], P('pipe', 'dp', 'tensor'), may hold values from -0.125 to 0.125
- value_matrix: bfloat16 [2, 2048, 512], P('pipe', 'dp', 'tensor'), may hold values from -0.125 to 0.125
- w_output: bfloat16 [2, 2048, 2048], P('pipe', 'tensor', 'dp'), may hold values from -1 to 1
- w_gate: bfloat16 [2, 2048, 8192], P('pipe', 'dp', 'tensor'), may hold values from -0.125 to 0.125
- w_up: bfloat16 [2, 2048, 8192], P('pipe', 'dp', 'tensor'), may hold values from -0.125 to 0.125
- w_down: bfloat16 [2, 8192, 2048], P('pipe', 'tensor', 'dp'), may hold values from -0.125 to 0.125
Outputs:
- layer_out: bfloat16 [2, 2, 1024, 2048], P('pipe', None, ('dp', 'tensor'))
- input_grad: bfloat16 [2, 2, 1024, 2048], P('pipe', None, ('dp', 'tensor'))
- grad_norm_gains: float32 [2, 2, 2048], P('pipe', None, ('dp', 'tensor'))
- grad_w_query: float32 [2, 2048, 2048], P('pipe', 'dp', 'tensor')
- grad_w_key: float32 [2, 2048, 512], P('pipe', 'dp', 'tensor')
- grad_w_value: float32 [2, 2048, 512], P('pipe', 'dp', 'tensor')
- grad_w_output: float32 [2, 2048, 2048], P('pipe', 'tensor', 'dp')
- grad_w_gate: float32 [2, 2048, 8192], P('pipe', 'dp', 'tensor')
- grad_w_up: float32 [2, 2048, 8192], P('pipe', 'dp', 'tensor')
- grad_w_down: float32 [2, 8192, 2048], P('pipe', 'tensor', 'dp')
Inputs may be any that keep to these rules, and one draw needn't show every extreme that they name: `segments`: document numbers never fall along a sequence; each of the 4 documents holds 1 to 512 consecutive tokens, one exactly 512.
All inputs are finite; a program needn't handle non-finite values.
Results may differ from a plain program's by a relative error of at most 0.03.
Values may be sent and summed in bfloat16 or wider, within the bound.
No kernel may reach another device: no remote copies, remote signals or barrier semaphores. Data moves between devices by JAX's collectives and lax.ppermute only.
A program may use at most 256 MiB of HBM per device.

v0:
```python
import jax
import jax.numpy as jnp
from jax import lax
from jax.experimental import pallas as pl
from jax.experimental.pallas import tpu as pltpu
from jax.sharding import Mesh, PartitionSpec as P

HEAD_SIZE = 64
KV_HEADS = 8
EPS = 1e-05
ROPE_BASE = 500000.0
NEG_FILL = -1e30
BF = jnp.bfloat16
F32 = jnp.float32
CUBE = ("wd", "tensor")


def rms_scale(row_values):
    return lax.rsqrt(jnp.mean(row_values * row_values, axis=-1, keepdims=True) + EPS)


def apply_norm(row_values, gain_vector):
    return row_values * rms_scale(row_values) * gain_vector


def norm_back(row_values, gain_vector, grad_normed):
    _, pullback = jax.vjp(apply_norm, row_values, gain_vector)
    return pullback(grad_normed)


def doc_starts(seg_row):
    places = jnp.arange(seg_row.shape[0], dtype=jnp.int32)
    before = jnp.concatenate([seg_row[:1] - 1, seg_row[:-1]])
    return lax.cummax(jnp.where(seg_row != before, places, 0), axis=0)


def rope_tables(positions):
    half_dim = HEAD_SIZE // 2
    freqs = ROPE_BASE ** (-(jnp.arange(half_dim, dtype=F32) * 2.0 / HEAD_SIZE))
    angles = positions.astype(F32)[:, None] * freqs[None, :]
    return (jnp.cos(angles), jnp.sin(angles))


def rotary_apply(head_values, cosine_table, sine_values):
    half_dim = head_values.shape[-1] // 2
    first_half = head_values[..., :half_dim]
    second_half = head_values[..., half_dim:]
    cos_rows = cosine_table[:, None, :]
    sin_rows = sine_values[:, None, :]
    return jnp.concatenate(
        [
            first_half * cos_rows - second_half * sin_rows,
            second_half * cos_rows + first_half * sin_rows,
        ],
        axis=-1,
    )


def mm(left, right):
    return jnp.dot(left, right, preferred_element_type=F32)


def mm_t(left, right):
    return lax.dot_general(left, right, (((1,), (1,)), ((), ())), preferred_element_type=F32)


def mm_tl(left, right):
    return lax.dot_general(left, right, (((0,), (0,)), ((), ())), preferred_element_type=F32)


def trade(blocks, axes):
    return lax.all_to_all(blocks, axes, 0, 0, tiled=True)


def hop(block, axis, step):
    size = lax.axis_size(axis)
    return lax.ppermute(block, axis, [(i, i ^ step) for i in range(size)])


def tie(*values):
    return lax.optimization_barrier(values)


def link_steps():
    steps = []
    step = 1
    while step < lax.axis_size(CUBE):
        steps.append(step)
        step *= 2
    return steps


FAR, NEAR, SIDE = 4, 2, 1
ROW_ORDER = (0, FAR, NEAR, FAR | NEAR, SIDE, FAR | SIDE, NEAR | SIDE, FAR | NEAR | SIDE)


def cube(block, step):
    return hop(block, CUBE, step)


def join_kernel(left_ref, left_came_ref, right_ref, right_came_ref, out_ref):
    half = left_ref.shape[1]
    block = pl.program_id(0)

    @pl.when(block < 2)
    def _():
        out_ref[:, :half] = left_ref[...]

    @pl.when(block >= 2)
    def _():
        out_ref[:, :half] = left_came_ref[...]

    @pl.when(block % 2 == 0)
    def _():
        out_ref[:, half:] = right_ref[...]

    @pl.when(block % 2 == 1)
    def _():
        out_ref[:, half:] = right_came_ref[...]


def join_halves(left, left_came, right, right_came):
    rows, half = left.shape[0] // 2, left.shape[1]

    def spec(place):
        return pl.BlockSpec((rows, half), lambda i: (place(i), 0))

    return pl.pallas_call(
        join_kernel,
        grid=(4,),
        in_specs=[
            spec(lambda i: jnp.minimum(i, 1)),
            spec(lambda i: jnp.maximum(i - 2, 0)),
            spec(lambda i: i // 2),
            spec(lambda i: i // 2),
        ],
        out_specs=pl.BlockSpec((rows, 2 * half), lambda i: (i, 0)),
        out_shape=jax.ShapeDtypeStruct((4 * rows, 2 * half), left.dtype),
        cost_estimate=pl.CostEstimate(
            flops=0, bytes_accessed=32 * rows * half, transcendentals=0
        ),
    )(left, left_came, right, right_came)


def gather_rows(rows):
    two = jnp.concatenate([rows, cube(rows, FAR)], axis=0)
    half = two.shape[1] // 2
    left, right = two[:, :half], two[:, half:]
    left_came, right_came = cube(left, NEAR), cube(right, SIDE)
    left = jnp.concatenate([left, left_came], axis=0)
    right = jnp.concatenate([right, right_came], axis=0)
    return join_halves(left, cube(left, SIDE), right, cube(right, NEAR))


def sum_rows(partial):
    partial = partial.astype(BF)
    n, half = partial.shape[0] // 4, partial.shape[1] // 2
    left, right = partial[:, :half], partial[:, half:]
    left_came = cube(left[2 * n :], SIDE)
    right_came = cube(jnp.concatenate([right[n : 2 * n], right[3 * n :]], axis=0), NEAR)
    left = left[: 2 * n].astype(F32) + left_came.astype(F32)
    right_came = right_came.astype(F32)
    low = right[:n].astype(F32) + right_came[:n]
    high = right[2 * n : 3 * n].astype(F32) + right_came[n:]
    left_came = cube(left[n:].astype(BF), NEAR)
    right_came = cube(high.astype(BF), SIDE)
    left = left[:n] + left_came.astype(F32)
    right = low + right_came.astype(F32)
    both = jnp.concatenate([left, right], axis=1)
    rows = n // 2
    return both[:rows] + cube(both[rows:].astype(BF), FAR).astype(F32)


class Stages:
    def __init__(self):
        self.held = {}
        self.then = {}

    def run(self, value, step, jobs, settle=()):
        needed = [[self.held[name] for name in job[2]] for job in jobs]
        value, needed = lax.optimization_barrier((value, needed))
        out = step(value)
        made = [job[1](*inputs) for job, inputs in zip(jobs, needed)]
        due = [m for m, job in zip(made, jobs) if len(job) == 3]
        ready = [self.held[key] for key in settle]
        out, due, ready = lax.optimization_barrier((out, due, ready))
        self.held.update(zip(settle, ready))
        for job, result in zip(jobs, made):
            self.held[job[0]] = due.pop(0) if len(job) == 3 else result
            if job[0] in self.then:
                self.then[job[0]](job[0])
        return out


def others(block, axis):
    return [block] + [hop(block, axis, k) for k in range(1, lax.axis_size(axis))]


def sum_others(blocks, axis):
    total = blocks[0].astype(F32)
    for k in range(1, lax.axis_size(axis)):
        total = total + hop(blocks[k].astype(BF), axis, k).astype(F32)
    return total


def relative(values, dim, axis):
    count = lax.axis_size(axis)
    me = lax.axis_index(axis)
    step = 1
    while step < count:
        shape = values.shape
        cut = shape[:dim] + (count // (2 * step), 2, step * (shape[dim] // count)) + shape[dim + 1 :]
        view = values.reshape(cut)
        swapped = jnp.concatenate(
            [lax.slice_in_dim(view, 1, 2, axis=dim + 1), lax.slice_in_dim(view, 0, 1, axis=dim + 1)],
            axis=dim + 1,
        )
        values = jnp.where((me & step) != 0, swapped.reshape(shape), values)
        step *= 2
    return values


def spread_gains(norm_gains):
    me = lax.axis_index(CUBE)
    gain = norm_gains
    for step in link_steps():
        came = hop(gain, CUBE, step)
        gain = jnp.where(
            (me & step) != 0,
            jnp.concatenate([came, gain], axis=1),
            jnp.concatenate([gain, came], axis=1),
        )
    gain = relative(jnp.concatenate(others(gain, "grp"), axis=1), 1, "grp")
    other = hop(gain, "pipe", 1)
    core = lax.axis_index("pipe")
    return [jnp.where(core == 0, gain, other), jnp.where(core == 0, other, gain)]


def sum_gains(grads):
    me = lax.axis_index(CUBE)
    keep, extra = own_layer(grads[0], grads[1])
    count = lax.axis_size("grp")
    total = relative((keep + extra).reshape(2, count, -1), 1, "grp")
    mine = total[:, 0]
    for k in range(1, count):
        mine = mine + hop(total[:, k], "grp", k)
    for step in link_steps()[::-1]:
        half = mine.shape[1] // 2
        low, high = mine[:, :half], mine[:, half:]
        odd = (me & step) != 0
        mine = jnp.where(odd, high, low) + hop(jnp.where(odd, low, high), CUBE, step)
    return mine


def masked_probs(q, k, q_place, q_start, k_place):
    scores = lax.dot_general(q, k, (((1,), (1,)), ((), ())), preferred_element_type=F32)
    scores = scores * HEAD_SIZE ** (-0.5)
    allowed = (k_place <= q_place) & (k_place >= q_start)
    masked = jnp.where(allowed, scores, NEG_FILL)
    exps = jnp.exp(masked - jnp.max(masked, axis=-1, keepdims=True))
    return exps / jnp.sum(exps, axis=-1, keepdims=True)


def attend_kernel(q_ref, k_ref, v_ref, qp_ref, qs_ref, kp_ref, o_ref):
    probs = masked_probs(q_ref[0], k_ref[...], qp_ref[...], qs_ref[...], kp_ref[...])
    o_ref[0] = jnp.dot(probs.astype(BF), v_ref[...], preferred_element_type=F32).astype(BF)


def attend_back_kernel(q_ref, do_ref, k_ref, v_ref, qp_ref, qs_ref, kp_ref, dq_ref, dk_ref, dv_ref):
    @pl.when((pl.program_id(0) == 0) & (pl.program_id(1) == 0))
    def _():
        dk_ref[...] = jnp.zeros_like(dk_ref)
        dv_ref[...] = jnp.zeros_like(dv_ref)

    q = q_ref[0]
    do = do_ref[0]
    k = k_ref[...]
    probs = masked_probs(q, k, qp_ref[...], qs_ref[...], kp_ref[...])
    grad_probs = lax.dot_general(do, v_ref[...], (((1,), (1,)), ((), ())), preferred_element_type=F32)
    delta = jnp.sum(probs * grad_probs, axis=-1, keepdims=True)
    grad_scores = (probs * (grad_probs - delta) * HEAD_SIZE ** (-0.5)).astype(BF)
    dq_ref[0] = jnp.dot(grad_scores, k, preferred_element_type=F32).astype(BF)
    dk_ref[...] += lax.dot_general(
        grad_scores, q, (((0,), (0,)), ((), ())), preferred_element_type=F32
    )
    dv_ref[...] += lax.dot_general(
        probs.astype(BF), do, (((0,), (0,)), ((), ())), preferred_element_type=F32
    )


def attention_specs(heads, rows, keys):
    rows_blk = max(16, min(rows, (512 * 1024) // keys))
    per_head = pl.BlockSpec((1, rows_blk, HEAD_SIZE), lambda b, h: (h, b, 0))
    full = pl.BlockSpec((keys, HEAD_SIZE), lambda b, h: (0, 0))
    row_info = pl.BlockSpec((rows_blk, 1), lambda b, h: (b, 0))
    key_info = pl.BlockSpec((1, keys), lambda b, h: (0, 0))
    return ((rows // rows_blk, heads), per_head, full, row_info, key_info)


PARAMS = dict(
    compiler_params=pltpu.CompilerParams(vmem_limit_bytes=50 * 1024 * 1024),
)


def attend(q, k, v, q_place, q_start, k_place):
    heads, rows, _ = q.shape
    keys = k.shape[0]
    grid, per_head, full, row_info, key_info = attention_specs(heads, rows, keys)
    return pl.pallas_call(
        attend_kernel,
        grid=grid,
        in_specs=[per_head, full, full, row_info, row_info, key_info],
        out_specs=per_head,
        out_shape=jax.ShapeDtypeStruct(q.shape, BF),
        cost_estimate=pl.CostEstimate(
            flops=4 * heads * rows * keys * HEAD_SIZE,
            bytes_accessed=4 * q.size + 4 * k.size,
            transcendentals=heads * rows * keys,
        ),
        **PARAMS,
    )(q, k, v, q_place, q_start, k_place)


def attend_back(q, do, k, v, q_place, q_start, k_place):
    heads, rows, _ = q.shape
    keys = k.shape[0]
    grid, per_head, full, row_info, key_info = attention_specs(heads, rows, keys)
    return pl.pallas_call(
        attend_back_kernel,
        grid=grid,
        in_specs=[per_head, per_head, full, full, row_info, row_info, key_info],
        out_specs=[per_head, full, full],
        out_shape=[
            jax.ShapeDtypeStruct(q.shape, BF),
            jax.ShapeDtypeStruct(k.shape, F32),
            jax.ShapeDtypeStruct(k.shape, F32),
        ],
        cost_estimate=pl.CostEstimate(
            flops=10 * heads * rows * keys * HEAD_SIZE,
            bytes_accessed=6 * q.size + 12 * k.size,
            transcendentals=heads * rows * keys,
        ),
        **PARAMS,
    )(q, do, k, v, q_place, q_start, k_place)


def to_blocks(weight, cores):
    wd = lax.axis_size("wd")
    rows = weight.shape[0]
    cut = weight.reshape(rows, wd, cores, -1).transpose(2, 1, 0, 3)
    return cut.reshape((cores * wd, rows) + cut.shape[3:])


def columns_out(blocks):
    moved = trade(blocks, ("pipe", "wd"))
    return moved.reshape((2, -1) + moved.shape[2:])


def put_kernel(spots, *refs):
    pieces, out = refs[: len(spots)], refs[len(spots)]
    block = pl.program_id(0)
    for piece, (first, count, col, cols) in zip(pieces, spots):

        def put(piece=piece, col=col, cols=cols):
            out[:, col : col + cols] = piece[...]

        pl.when((block >= first) & (block < first + count))(put)


def put_together(columns):
    block = min([256] + [piece.shape[0] for stack in columns for piece in stack])
    spots, pieces, specs = [], [], []
    col = 0
    for stack in columns:
        first = 0
        for piece in stack:
            count, cols = piece.shape[0] // block, piece.shape[1]
            spots.append((first, count, col, cols))
            pieces.append(piece)

            def at(i, first=first, count=count):
                return (jnp.clip(i - first, 0, count - 1), 0)

            specs.append(pl.BlockSpec((block, cols), at))
            first += count
        col += cols
    return pl.pallas_call(
        lambda *refs: put_kernel(spots, *refs),
        grid=(first,),
        in_specs=specs,
        out_specs=pl.BlockSpec((block, col), lambda i: (i, 0)),
        out_shape=jax.ShapeDtypeStruct((first * block, col), BF),
        cost_estimate=pl.CostEstimate(
            flops=0, bytes_accessed=4 * first * block * col, transcendentals=0
        ),
        **PARAMS,
    )(*pieces)


def pack_attention(w_query, key_matrix, value_matrix, w_output, cores):
    wd = lax.axis_size("wd")
    rows = w_query.shape[0]
    cut = [w_query.reshape(rows, wd, cores, -1)]
    for m in (key_matrix, value_matrix):
        m = m.reshape(rows, wd, 1, -1)
        cut.append(jnp.broadcast_to(m, (rows, wd, cores, m.shape[3])))
    cut.append(w_output.T.reshape(rows, wd, cores, -1))
    return jnp.concatenate(cut, axis=-1).reshape(rows, -1)


def unpack_attention(own, widths):
    other = hop(own, "pipe", 1)
    query_w, kv_w, out_w = widths
    cuts = (query_w, query_w + kv_w, query_w + 2 * kv_w)
    return (
        jnp.concatenate([own[:, : cuts[0]], other[:, : cuts[0]]], axis=1),
        own[:, cuts[0] : cuts[1]],
        own[:, cuts[1] : cuts[2]],
        jnp.concatenate([own[:, cuts[2] :], other[:, cuts[2] :]], axis=1),
    )


def grad_pair(own, other):
    return (own + hop(other.astype(BF), "pipe", 1).astype(F32)).astype(BF)


def mlp_pair(left, right):
    half = right.shape[1] // 2
    return grad_pair(mm_tl(left, right[:, :half]), mm_tl(left, right[:, half:]))


def grad_group(total):
    return lax.psum_scatter(total, "grp", scatter_dimension=0, tiled=True)


def grad_home(total):
    return trade(total.reshape((lax.axis_size("wd"), -1) + total.shape[1:]), "wd")


def place_kernel(turned, at_ref, keep_ref, got_ref, out_ref):
    mine = pl.program_id(1) == at_ref[0]

    def put(ref):
        block = ref[0].astype(F32)
        out_ref[...] = block.T if turned else block

    @pl.when(mine)
    def _():
        put(keep_ref)

    @pl.when(jnp.logical_not(mine))
    def _():
        put(got_ref)


def place(keep, got, turned):
    wd, rows, cols = keep.shape
    at = lax.axis_index("pipe").astype(jnp.int32)[None]
    cores = lax.axis_size("pipe")
    source = pl.BlockSpec((1, rows, cols), lambda w, c, at_ref: (w, 0, 0))
    if turned:
        shape, target = (wd * cores * cols, rows), (cols, rows)
        out = pl.BlockSpec(target, lambda w, c, at_ref: (w * cores + c, 0))
    else:
        shape, target = (rows, wd * cores * cols), (rows, cols)
        out = pl.BlockSpec(target, lambda w, c, at_ref: (0, w * cores + c))
    return pl.pallas_call(
        lambda *refs: place_kernel(turned, *refs),
        grid_spec=pltpu.PrefetchScalarGridSpec(
            num_scalar_prefetch=1, grid=(wd, cores), in_specs=[source, source], out_specs=out
        ),
        out_shape=jax.ShapeDtypeStruct(shape, F32),
        cost_estimate=pl.CostEstimate(
            flops=keep.size, bytes_accessed=12 * keep.size, transcendentals=0
        ),
    )(at, keep, got)


def layer_forward(stages, layer, x_rows, gains, where, build, jobs, settle):
    held = stages.held
    cosine, sine, q_place, q_start, k_place = where
    normed = apply_norm(x_rows, gains[0]).astype(BF)
    rows_a = stages.run(normed, gather_rows, jobs[0], settle[0])
    held["attn", layer] = build("attn", layer)
    w_q, w_k, w_v, w_ot = held["attn", layer]
    tok = rows_a.shape[0]

    def project(rows):
        key = rotary_apply(mm(rows, w_k).reshape(tok, 1, HEAD_SIZE), cosine, sine).astype(BF)[:, 0]
        value = mm(rows, w_v).astype(BF)
        return jnp.concatenate([key, value], axis=1)

    def queries(rows):
        query = rotary_apply(mm(rows, w_q).reshape(tok, -1, HEAD_SIZE), cosine, sine).astype(BF)
        return query.transpose(1, 0, 2)

    held["rows_a"] = rows_a
    kv_all = stages.run(
        project(rows_a),
        lambda kv: jnp.concatenate(others(kv, "grp"), axis=0),
        [("query", queries, ("rows_a",))] + jobs[1],
        settle[1],
    )
    query = held["query"]
    keys, values = kv_all[:, :HEAD_SIZE], kv_all[:, HEAD_SIZE:]

    def attention(q):
        context = attend(q, keys, values, q_place, q_start, k_place)
        context = context.transpose(1, 0, 2).reshape(tok, -1)
        return context, mm_t(context, w_ot).astype(BF)

    context, partial = stages.run(query, attention, jobs[2], settle[2])
    mid = stages.run(partial, lambda p: x_rows + sum_rows(p), jobs[3], settle[3])
    rows_b = stages.run(
        mid, lambda m: gather_rows(apply_norm(m, gains[1]).astype(BF)), jobs[4], settle[4]
    )
    held["gu", layer] = w_gu = build("gu", layer)

    def ahead(rows):
        both = mm(rows, w_gu)
        half = both.shape[1] // 2
        gate, up = both[:, :half], both[:, half:]
        return gate, up, (jax.nn.silu(gate) * up).astype(BF)

    gate, up, hidden = stages.run(rows_b, ahead, jobs[5], settle[5])
    held["down", layer] = build("down", layer)
    return x_rows, rows_a, query, keys, values, context, mid, rows_b, gate, up, hidden


def layer_backward(
    stages, layer, grad_out, grad_mlp, gains, where, kept, also, jobs, settle
):
    held = stages.held
    cosine, sine, q_place, q_start, k_place = where
    x_rows, rows_a, query, keys, values, context, mid, rows_b, gate, up, hidden = kept
    w_q, w_k, w_v, w_ot = held["attn", layer]
    w_gu, w_dt = held["gu", layer], held["down", layer]
    tok = rows_a.shape[0]
    held["rows_b"], held["hidden"], held["grad_mlp"] = rows_b, hidden, grad_mlp

    def feed_back(rows):
        grad_hidden = mm(rows, w_dt)
        sig = jax.nn.sigmoid(gate)
        grad_gate = (grad_hidden * up * sig * (1.0 + gate * (1.0 - sig))).astype(BF)
        grad_up = (grad_hidden * gate * sig).astype(BF)
        both = jnp.concatenate([grad_gate, grad_up], axis=1)
        return grad_gate, grad_up, mm_t(both, w_gu).astype(BF), also(hidden)

    grad_gate, grad_up, partial, extra = stages.run(grad_mlp, feed_back, jobs[0], settle[0])
    held["grad_gate"], held["grad_up"] = grad_gate, grad_up
    grad_b = stages.run(partial, sum_rows, jobs[1], settle[1])
    grad_mid, gain_b = norm_back(mid, gains[1], grad_b)
    grad_mid = grad_mid + grad_out
    grad_attn = stages.run(grad_mid.astype(BF), gather_rows, jobs[2], settle[2])

    def attention_back(rows):
        grad_context = mm(rows, w_ot).astype(BF)
        grad_context = grad_context.reshape(tok, -1, HEAD_SIZE).transpose(1, 0, 2)
        return attend_back(query, grad_context, keys, values, q_place, q_start, k_place)

    def keys_back(grads):
        kv = jnp.concatenate(grads, axis=1)
        kv = kv.reshape((-1, tok) + kv.shape[1:])
        return sum_others([kv[k] for k in range(kv.shape[0])], "grp").astype(BF)

    def queries_back(grad_q):
        grad_q = grad_q.transpose(1, 0, 2).astype(F32)
        grad_q = rotary_apply(grad_q, cosine, -sine).astype(BF).reshape(tok, -1)
        return grad_q, mm_t(grad_q, w_q)

    held["grad_q"], *grads = stages.run(grad_attn, attention_back, jobs[3])
    own_kv = stages.run(
        grads, keys_back, [("g_q", queries_back, ("grad_q",))] + jobs[4], settle[4]
    )
    grad_q, partial = held["g_q"]
    grad_k = own_kv[:, :HEAD_SIZE].astype(F32)
    grad_k = rotary_apply(grad_k[:, None, :], cosine, -sine).astype(BF)[:, 0]
    grad_v = own_kv[:, HEAD_SIZE:]
    partial = (partial + mm_t(grad_k, w_k) + mm_t(grad_v, w_v)).astype(BF)

    def attn_pair(g_q, g_k, g_v):
        half_q = g_q.shape[1] // 2

        def term(cut):
            right = jnp.concatenate([g_q[:, cut], g_k, g_v], axis=1)
            left = [mm_tl(rows_a, right), mm_tl(grad_attn, context[:, cut])]
            return jnp.concatenate(left, axis=1)

        return grad_pair(term(slice(0, half_q)), term(slice(half_q, None)))

    held["g_q"], held["g_k"], held["g_v"] = grad_q, grad_k, grad_v
    grad_a = stages.run(partial, sum_rows, jobs[5](attn_pair), settle[5])
    grad_in, gain_a = norm_back(x_rows, gains[0], grad_a)
    return grad_mid + grad_in, jnp.stack([gain_a, gain_b]), extra


def own_layer(first, second):
    core = lax.axis_index("pipe")
    keep = jnp.where(core == 0, first, second)
    return keep, hop(jnp.where(core == 0, second, first), "pipe", 1)


def body(
    block_input,
    cotangent,
    segments,
    norm_gains,
    w_query,
    key_matrix,
    value_matrix,
    w_output,
    w_gate,
    w_up,
    w_down,
):
    core = lax.axis_index("pipe")
    grp = lax.axis_index("grp")
    wd = lax.axis_size("wd")
    groups = lax.axis_size("grp")
    cores = lax.axis_size("pipe")
    tok = block_input.shape[1] * lax.axis_size(CUBE)

    stages = Stages()
    held = stages.held
    packed = pack_attention(w_query[0], key_matrix[0], value_matrix[0], w_output[0], cores)
    gains = spread_gains(norm_gains[0])
    packed, gains = lax.optimization_barrier((packed, gains))
    attn_cols = columns_out(to_blocks(packed, cores))
    held["gate_out"] = to_blocks(w_gate[0], cores)
    held["up_out"] = to_blocks(w_up[0], cores)
    held["down_out"] = to_blocks(w_down[0].T, cores)
    query_w, out_w = w_query.shape[2] // (wd * cores), w_output.shape[1] // (wd * cores)
    widths = (query_w, key_matrix.shape[2] // wd, out_w)

    def move(name):
        return (name, columns_out, (name + "_out",), "later")

    def rows_of(name, layer):
        return lax.all_gather(held[name][layer], "grp", axis=0, tiled=True)

    def put(*names):
        return put_together([[m] for n in names for m in (held[n], hop(held[n], "pipe", 1))])

    def build(kind, layer):
        if kind == "attn":
            return unpack_attention(held["own", "attn", layer], widths)
        if kind == "gu":
            return put(("own", "gate", layer), ("own", "up", layer))
        return put(("own", "down", layer))

    held["attn"] = attn_cols
    for layer in range(2):
        held["own", "attn", layer] = rows_of("attn", layer)

    def start(name):
        for layer in range(2):
            held["own", name, layer] = rows_of(name, layer)

    stages.then.update(gate=start, up=start, down=start)

    seg_row = lax.dynamic_index_in_dim(segments, core, 0, keepdims=False)
    starts = doc_starts(seg_row)
    rows_own = tok // lax.axis_size(CUBE)

    def in_row_order(values):
        values = relative(values, 0, CUBE)
        return jnp.concatenate(
            [values[j * rows_own : (j + 1) * rows_own] for j in ROW_ORDER], axis=0
        )

    local = in_row_order(jnp.arange(tok, dtype=jnp.int32))
    q_place = grp * tok + local
    q_start = in_row_order(lax.dynamic_slice_in_dim(starts, grp * tok, tok))
    cosine, sine = rope_tables(q_place - q_start)
    k_place = jnp.concatenate([(grp ^ k) * tok + local for k in range(groups)])
    where = (cosine, sine, q_place[:, None], q_start[:, None], k_place[None, :])

    rows = lax.dynamic_index_in_dim(block_input, core, 0, keepdims=False)
    grad = lax.dynamic_index_in_dim(cotangent, core, 0, keepdims=False)
    held["cotangent"] = grad
    kept = [None, None]
    outs = [None, None]
    kept[0] = layer_forward(
        stages,
        0,
        rows.astype(F32),
        gains[0],
        where,
        build,
        [
            [],
            [move("gate")],
            [move("up"), ("last", gather_rows, ("cotangent",))],
            [move("down")],
            [],
            [],
        ],
        [
            (),
            (("own", "attn", 1),),
            (("own", "gate", 0),),
            (("own", "up", 0),),
            (("own", "down", 0),),
            (),
        ],
    )

    def close(hidden, layer):
        return (kept[layer][6] + sum_rows(mm_t(hidden, held["down", layer]))).astype(BF)

    outs[0] = stages.run(
        kept[0][-1], lambda h: close(h, 0), [], (("own", "gate", 1),)
    )
    kept[1] = layer_forward(
        stages,
        1,
        outs[0].astype(F32),
        gains[1],
        where,
        build,
        [[]] * 6,
        [(("own", "up", 1),), (), (("own", "down", 1),), (), (), ()],
    )

    def grad_of(name, layer):
        sources = {
            "down": ("grad_mlp", "hidden"),
            "gate": ("rows_b", "grad_gate"),
            "up": ("rows_b", "grad_up"),
        }[name]
        return (("pair", name, layer), mlp_pair, sources)

    def group_sum(name, layer):
        return (("sum", name, layer), grad_group, (("pair", name, layer),), "later")

    def home(name, layer):
        return (("home", name, layer), grad_home, (("sum", name, layer),), "later")

    def attn_grad(layer):
        return lambda pair: (("pair", "attn", layer), pair, ("g_q", "g_k", "g_v"))

    def final(name, turned):
        def ready(first, second):
            return place(*own_layer(first, second), turned)

        return (("final", name), ready, (("home", name, 0), ("home", name, 1)))

    held["hidden"], held["grad_mlp"] = kept[1][-1], held["last"]
    hidden = stages.run(kept[1][-1], lambda h: h, [grad_of("down", 1)])

    grads_in = [None, None]
    gain_grads = [None, None]
    grad_in, gain_grads[1], outs[1] = layer_backward(
        stages,
        1,
        grad.astype(F32),
        held["last"],
        gains[1],
        where,
        kept[1][:-1] + (hidden,),
        lambda h: close(h, 1),
        (
            [],
            [group_sum("down", 1), grad_of("gate", 1)],
            [group_sum("gate", 1), grad_of("up", 1)],
            [group_sum("up", 1)],
            [home("down", 1)],
            lambda pair: [attn_grad(1)(pair)],
        ),
        [(), (), (), (), (), (("sum", "gate", 1), ("home", "down", 1))],
    )
    grads_in[1] = grad_in.astype(BF)
    grad_mlp = stages.run(grads_in[1], gather_rows, [group_sum("attn", 1)], (("sum", "up", 1),))
    grad_in, gain_grads[0], _ = layer_backward(
        stages,
        0,
        grads_in[1].astype(F32),
        grad_mlp,
        gains[0],
        where,
        kept[0],
        lambda h: (),
        (
            [grad_of("down", 0), home("gate", 1)],
            [group_sum("down", 0), grad_of("gate", 0), home("up", 1)],
            [group_sum("gate", 0), grad_of("up", 0), home("attn", 1)],
            [group_sum("up", 0)],
            [home("down", 0)],
            lambda pair: [attn_grad(0)(pair)],
        ),
        [
            (),
            (("sum", "attn", 1), ("home", "gate", 1)),
            (("sum", "down", 0), ("home", "up", 1)),
            (),
            (("sum", "gate", 0), ("home", "attn", 1)),
            (("sum", "up", 0), ("home", "down", 0)),
        ],
    )
    grads_in[0] = grad_in.astype(BF)
    for key, job, names, *_ in (
        group_sum("attn", 0),
        home("gate", 0),
        final("down", True),
        final("gate", False),
        home("up", 0),
        final("up", False),
    ):
        held[key] = job(*[held[name] for name in names])
    keys = (("sum", "attn", 0),) + tuple(("final", name) for name in ("down", "gate", "up"))
    held.update(zip(keys, lax.optimization_barrier([held[key] for key in keys])))
    key, job, *_ = home("attn", 0)
    held[key] = job(held["sum", "attn", 0])

    def by_batch(pair):
        own, other = own_layer(pair[0], pair[1])
        both = jnp.where(core == 0, jnp.stack([own, other]), jnp.stack([other, own]))
        return both[None]

    layer_out = by_batch(outs)
    input_grad = by_batch(grads_in)

    grad_norm_gains = sum_gains(gain_grads)[None]

    def both(name):
        return own_layer(held["home", name, 0], held["home", name, 1])

    keep, got = both("attn")
    cuts = (0, widths[0], widths[0] + widths[1], widths[0] + 2 * widths[1], keep.shape[2])
    q_pair, k_pair, v_pair, o_pair = (
        (keep[..., lo:hi], got[..., lo:hi]) for lo, hi in zip(cuts[:-1], cuts[1:])
    )

    def small(pair):
        order = pair[0].transpose(1, 0, 2).astype(F32)
        return order.reshape(order.shape[0], -1)[None]

    grad_wq = place(*q_pair, False)[None]
    grad_wk = small(k_pair)
    grad_wv = small(v_pair)
    grad_wo = place(*o_pair, True)[None]
    grad_wg = held["final", "gate"][None]
    grad_wu = held["final", "up"][None]
    grad_wd = held["final", "down"][None]
    return (
        layer_out,
        input_grad,
        grad_norm_gains,
        grad_wq,
        grad_wk,
        grad_wv,
        grad_wo,
        grad_wg,
        grad_wu,
        grad_wd,
    )


def solution(mesh):
    sizes = dict(mesh.shape)
    wd = KV_HEADS // sizes["tensor"]
    fine = Mesh(
        mesh.devices.reshape(sizes["pipe"], sizes["dp"] // wd, wd, sizes["tensor"]),
        ("pipe", "grp", "wd", "tensor"),
    )
    dp = ("grp", "wd")
    tokens = P(None, dp + ("tensor",), None)
    outs = P("pipe", None, dp + ("tensor",), None)
    gains = P("pipe", None, dp + ("tensor",))
    tall = P("pipe", dp, "tensor")
    wide = P("pipe", "tensor", dp)
    weights = (tall, tall, tall, wide, tall, tall, wide)
    return jax.shard_map(
        body,
        mesh=fine,
        in_specs=(tokens, tokens, P(), gains) + weights,
        out_specs=(outs, outs, gains) + weights,
        check_vma=False,
    )
```

profile of v0, /device:TPU:0, one launch (start us, length us, event | category | flops | bytes accessed | tf_op | source)
XLA Modules:
  0.0 1216.2 jit_solution(2696671001711964341)
XLA Ops:
  38.5 15.2 %all-to-all-done = bf16[8,256,384]{2,1,0:T(8,128)(2,1)S(1)} async-done(((bf16[8,256,384]{2,1,0:T(8,128)(2,1)}), bf16[8,256,384]{2,1,0:T(8,128)(2,1)S(1)}, u32[]{:S(2)}, u32[]{:S(2)}) %all-to-all-start) | async-done | bytes 1572896 | tf_op jit(solution)/shard_map/all_to_all | solution.py:72
  68.2 6.9 collective-permute-done.8
  77.2 7.5 collective-permute-done.7.left_came_ref
  90.6 8.9 all-gather.9.cloned.1.call-done
  123.0 21.1 %collective-permute-done.10 = bf16[512,128]{1,0:T(8,128)(2,1)S(1)} collective-permute-done((bf16[512,128]{1,0:T(8,128)(2,1)S(1)}, bf16[512,128]{1,0:T(8,128)(2,1)S(1)}, u32[]{:S(2)}, u32[]{:S(2)}) %collective-permute-start.10) | collective-permute-done | bytes 131104 | tf_op jit(solution)/shard_map/ppermute | solution.py:77
  148.3 19.7 %all-gather.11.cloned.1.call-done = bf16[2048,384]{1,0:T(8,128)(2,1)} async-done(((bf16[1024,384]{1,0:T(8,128)(2,1)}), bf16[2048,384]{1,0:T(8,128)(2,1)}) %all-gather.11.cloned.1.call-update) | async-done | bytes 1572880 | tf_op jit(solution)/shard_map/all_gather | solution.py:639
  178.1 41.8 %collective-permute-done.12 = bf16[64,2048]{1,0:T(8,128)(2,1)S(1)} collective-permute-done((bf16[64,2048]{1,0:T(8,128)(2,1)S(1)}, bf16[64,2048]{1,0:T(8,128)(2,1)S(1)}, u32[]{:S(2)}, u32[]{:S(2)}) %collective-permute-start.12) | collective-permute-done | bytes 262176 | tf_op jit(solution)/shard_map/ppermute | solution.py:77
  232.6 7.1 shard_map.187
  259.4 8.1 collective-permute-done.17
  270.5 18.9 %collective-permute-done.19 = bf16[256,1024]{1,0:T(8,128)(2,1)S(1)} collective-permute-done((bf16[256,1024]{1,0:T(8,128)(2,1)}, bf16[256,1024]{1,0:T(8,128)(2,1)S(1)}, u32[]{:S(2)}, u32[]{:S(2)}) %collective-permute-start.19) | collective-permute-done | bytes 524320 | tf_op jit(solution)/shard_map/ppermute | solution.py:77
  299.9 19.7 %collective-permute-done.21 = bf16[64,2048]{1,0:T(8,128)(2,1)S(1)} collective-permute-done((bf16[64,2048]{1,0:T(8,128)(2,1)S(1)}, bf16[64,2048]{1,0:T(8,128)(2,1)S(1)}, u32[]{:S(2)}, u32[]{:S(2)}) %collective-permute-start.21) | collective-permute-done | bytes 262176 | tf_op jit(solution)/shard_map/ppermute | solution.py:77
  323.2 8.7 collective-permute-done.22
  335.0 5.0 collective-permute-done.23
  343.9 9.7 collective-permute-done.24.left_came_ref
  358.8 19.1 %all-gather.17.cloned.1.call-done.refs_0_ = bf16[2048,512]{1,0:T(8,128)(2,1)} async-done(((bf16[1024,512]{1,0:T(8,128)(2,1)}), bf16[2048,512]{1,0:T(8,128)(2,1)}) %all-gather.17.cloned.1.call-update) | async-done | bytes 2097168 | tf_op jit(solution)/shard_map/all_gather | solution.py:639
  378.0 8.3 shard_map.190
  386.4 7.3 fusion.248
  396.8 6.2 shard_map.191
  410.8 11.3 collective-permute-done.30
  425.5 4.9 collective-permute-done.31
  432.2 8.6 collective-permute-done.34
  441.9 9.2 collective-permute-done.35
  477.0 16.3 %all-gather.21.cloned.1.call-done.refs_2_ = bf16[2048,512]{1,0:T(8,128)(2,1)} async-done(((bf16[1024,512]{1,0:T(8,128)(2,1)}), bf16[2048,512]{1,0:T(8,128)(2,1)}) %all-gather.21.cloned.1.call-update) | async-done | bytes 2097168 | tf_op jit(solution)/shard_map/all_gather | solution.py:639
  506.3 28.4 %collective-permute-done.40 = bf16[512,128]{1,0:T(8,128)(2,1)S(1)} collective-permute-done((bf16[512,128]{1,0:T(8,128)(2,1)}, bf16[512,128]{1,0:T(8,128)(2,1)S(1)}, u32[]{:S(2)}, u32[]{:S(2)}) %collective-permute-start.40) | collective-permute-done | bytes 131104 | tf_op jit(solution)/shard_map/ppermute | solution.py:77
  535.8 7.1 shard_map.193
  546.4 8.2 all-gather.23.cloned.1.call-done.refs_0_
  559.9 9.8 collective-permute-done.43
  580.2 6.0 collective-permute-done.47
  586.7 6.4 collective-permute-done.48
  595.0 6.1 collective-permute-done.49
  607.1 8.1 shard_map.196
  619.9 7.7 fusion.249
  632.6 6.0 shard_map.194
  641.3 5.0 convolution_convert_fusion
  652.4 8.0 collective-permute-done.58
  662.9 5.2 collective-permute-done.59
  682.9 5.1 collective-permute-done.62
  698.3 10.6 collective-permute-done.66
  719.6 18.3 %collective-permute-done.68 = bf16[64,2048]{1,0:T(8,128)(2,1)S(1)} collective-permute-done((bf16[64,2048]{1,0:T(8,128)(2,1)S(1)}, bf16[64,2048]{1,0:T(8,128)(2,1)S(1)}, u32[]{:S(2)}, u32[]{:S(2)}) %collective-permute-start.68) | collective-permute-done | bytes 262176 | tf_op jit(solution)/shard_map/ppermute | solution.py:77
  740.9 5.4 collective-permute-done.69
  749.4 10.1 collective-permute-done.70.left_came_ref
  765.6 5.1 add_convert_fusion.5
  775.6 9.3 shard_map.198
  812.8 9.6 collective-permute-done.77
  835.0 24.7 %collective-permute-done.79 = bf16[64,2048]{1,0:T(8,128)(2,1)S(1)} collective-permute-done((bf16[64,2048]{1,0:T(8,128)(2,1)S(1)}, bf16[64,2048]{1,0:T(8,128)(2,1)S(1)}, u32[]{:S(2)}, u32[]{:S(2)}) %collective-permute-start.79) | collective-permute-done | bytes 262176 | tf_op jit(solution)/shard_map/ppermute | solution.py:77
  862.3 6.3 collective-permute-done.81
  872.0 6.2 collective-permute-done.82
  881.3 7.0 collective-permute-done.83.left_came_ref
  899.0 6.9 multiply_convert_fusion
  905.9 7.4 convolution_convert_fusion.7
  941.4 7.1 collective-permute-done.88
  950.1 12.0 collective-permute-done.91
  973.4 11.2 collective-permute-done.93
  1005.7 9.1 collective-permute-done.97.right_came_ref
  1018.7 5.1 add_convert_fusion.1
  1032.1 9.3 shard_map.201
  1068.2 11.8 collective-permute-done.102
  1097.3 12.5 %collective-permute-done.104 = bf16[64,2048]{1,0:T(8,128)(2,1)} collective-permute-done((bf16[64,2048]{1,0:T(8,128)(2,1)}, bf16[64,2048]{1,0:T(8,128)(2,1)}, u32[]{:S(2)}, u32[]{:S(2)}) %collective-permute-start.104) | collective-permute-done | bytes 262176 | tf_op jit(solution)/shard_map/ppermute | solution.py:77
  1129.1 15.7 %all-to-all-done.10 = bf16[4,256,512]{2,1,0:T(8,128)(2,1)} async-done(((bf16[4,256,512]{2,1,0:T(8,128)(2,1)}), bf16[4,256,512]{2,1,0:T(8,128)(2,1)}, u32[]{:S(2)}, u32[]{:S(2)}) %all-to-all-start.10) | async-done | bytes 1048608 | tf_op jit(solution)/shard_map/all_to_all | solution.py:72
  1151.4 6.4 shard_map.203
  1157.8 6.8 shard_map.202
  1165.7 6.4 shard_map.204
  1180.1 9.5 collective-permute-done.110
  1204.3 4.9 shard_map.206
  (953 shorter events, 536.5 us)
Async XLA Ops:
  29.3 24.4 %all-to-all-start = ((bf16[8,256,384]{2,1,0:T(8,128)(2,1)}), bf16[8,256,384]{2,1,0:T(8,128)(2,1)S(1)}, u32[]{:S(2)}, u32[]{:S(2)}) async-start(bf16[8,256,384]{2,1,0:T(8,128)(2,1)} %bitcast.250), calls=%async_computation | async-start | bytes 3145728 | tf_op jit(solution)/shard_map/all_to_all | solution.py:72
  33.2 66.3 %all-gather.9.cloned.1.call-start = ((), (), s32[]{:S(2)}) async-start(), calls=%async_computation.20 | async-start | bytes 2359296 | tf_op jit(solution)/shard_map/all_gather | solution.py:639
  36.5 22.5 %collective-permute-start.5 = (bf16[64,2048]{1,0:T(8,128)(2,1)S(1)}, bf16[64,2048]{1,0:T(8,128)(2,1)S(1)}, u32[]{:S(2)}, u32[]{:S(2)}) collective-permute-start(bf16[64,2048]{1,0:T(8,128)(2,1)S(1)} %fusion.16), channel_id=1, source_target_pairs={{0,4},{1,5},{2,6},{3,7},{4,0},{5,1},{6,2},{7,3},{8,12},{9,13},{10,... | collective-permute-start | bytes 786440 | tf_op jit(solution)/shard_map/ppermute | solution.py:77
  66.9 17.7 %collective-permute-start.7 = (bf16[256,1024]{1,0:T(8,128)(2,1)S(1)}, bf16[256,1024]{1,0:T(8,128)(2,1)S(1)}, u32[]{:S(2)}, u32[]{:S(2)}) collective-permute-start(bf16[256,1024]{1,0:T(8,128)(2,1)S(1)} %pad_maximum_fusion.23.left_ref), channel_id=1, source_target_pairs={{0,1},{1,0},{2,3},{3,2},{4,5},{5,4},{6,7},{7,6},{8,9},{9,8},{10,11... | collective-permute-start | bytes 1572872 | tf_op jit(solution)/shard_map/ppermute | solution.py:77
  105.4 62.7 %all-to-all-start.1 = ((bf16[8,256,512]{2,1,0:T(8,128)(2,1)}), bf16[8,256,512]{2,1,0:T(8,128)(2,1)}, u32[]{:S(2)}, u32[]{:S(2)}) async-start(bf16[8,256,512]{2,1,0:T(8,128)(2,1)} %bitcast.246), calls=%async_computation.1 | async-start | bytes 4194304 | tf_op jit(solution)/shard_map/all_to_all | solution.py:72
  109.7 58.3 %all-gather.11.cloned.1.call-start = ((), (), s32[]{:S(2)}) async-start(), calls=%async_computation.21 | async-start | bytes 2359296 | tf_op jit(solution)/shard_map/all_gather | solution.py:639
  109.8 34.3 %collective-permute-start.11 = (bf16[2048,384]{1,0:T(8,128)(2,1)}, bf16[2048,384]{1,0:T(8,128)(2,1)}, u32[]{:S(2)}, u32[]{:S(2)}) collective-permute-start(bf16[2048,384]{1,0:T(8,128)(2,1)} %all-gather.9.cloned.1.call-done), channel_id=1, source_target_pairs={{0,16},{16,0},{1,17},{17,1},{2,18},{18,2},{3,19},{19,3},{4,20},{20... | collective-permute-start | bytes 4718600 | tf_op jit(solution)/shard_map/ppermute | solution.py:77
  120.8 23.3 %collective-permute-start.10 = (bf16[512,128]{1,0:T(8,128)(2,1)S(1)}, bf16[512,128]{1,0:T(8,128)(2,1)S(1)}, u32[]{:S(2)}, u32[]{:S(2)}) collective-permute-start(bf16[512,128]{1,0:T(8,128)(2,1)S(1)} %pad_maximum_fusion.69), channel_id=1, source_target_pairs={{0,8},{8,0},{1,9},{9,1},{2,10},{10,2},{3,11},{11,3},{4,12},{12,4},... | collective-permute-start | bytes 393224 | tf_op jit(solution)/shard_map/ppermute | solution.py:77
  168.0 79.8 %all-to-all-start.2 = ((bf16[8,256,512]{2,1,0:T(8,128)(2,1)}), bf16[8,256,512]{2,1,0:T(8,128)(2,1)}, u32[]{:S(2)}, u32[]{:S(2)}) async-start(bf16[8,256,512]{2,1,0:T(8,128)(2,1)} %bitcast.32), calls=%async_computation.2 | async-start | bytes 4194304 | tf_op jit(solution)/shard_map/all_to_all | solution.py:72
  172.5 75.3 %all-gather.13.cloned.1.call-start = ((), (), s32[]{:S(2)}) async-start(), calls=%async_computation.22 | async-start | bytes 3145728 | tf_op jit(solution)/shard_map/all_gather | solution.py:639
  175.8 44.1 %collective-permute-start.12 = (bf16[64,2048]{1,0:T(8,128)(2,1)S(1)}, bf16[64,2048]{1,0:T(8,128)(2,1)S(1)}, u32[]{:S(2)}, u32[]{:S(2)}) collective-permute-start(bf16[64,2048]{1,0:T(8,128)(2,1)S(1)} %copy-done.108), channel_id=1, source_target_pairs={{0,4},{1,5},{2,6},{3,7},{4,0},{5,1},{6,2},{7,3},{8,12},{9,13},{10,... | collective-permute-start | bytes 786440 | tf_op jit(solution)/shard_map/ppermute | solution.py:77
  247.8 72.2 %all-to-all-start.3 = ((bf16[8,256,512]{2,1,0:T(8,128)(2,1)}), bf16[8,256,512]{2,1,0:T(8,128)(2,1)}, u32[]{:S(2)}, u32[]{:S(2)}) async-start(bf16[8,256,512]{2,1,0:T(8,128)(2,1)} %bitcast.51), calls=%async_computation.3 | async-start | bytes 4194304 | tf_op jit(solution)/shard_map/all_to_all | solution.py:72
  252.2 67.6 %all-gather.15.cloned.1.call-start = ((), (), s32[]{:S(2)}) async-start(), calls=%async_computation.23 | async-start | bytes 3145728 | tf_op jit(solution)/shard_map/all_gather | solution.py:639
  254.5 35.0 %collective-permute-start.19 = (bf16[256,1024]{1,0:T(8,128)(2,1)}, bf16[256,1024]{1,0:T(8,128)(2,1)S(1)}, u32[]{:S(2)}, u32[]{:S(2)}) collective-permute-start(bf16[256,1024]{1,0:T(8,128)(2,1)} %pad_maximum_fusion.27), channel_id=1, source_target_pairs={{0,2},{1,3},{2,0},{3,1},{4,6},{5,7},{6,4},{7,5},{8,10},{9,11},{10,... | collective-permute-start | bytes 1572872 | tf_op jit(solution)/shard_map/ppermute | solution.py:77
  259.4 118.6 %all-gather.17.cloned.1.call-start = ((), (), s32[]{:S(2)}) async-start(), calls=%async_computation.24 | async-start | bytes 3145728 | tf_op jit(solution)/shard_map/all_gather | solution.py:639
  268.8 25.8 %collective-permute-start.18 = (bf16[128,1024]{1,0:T(8,128)(2,1)S(1)}, bf16[128,1024]{1,0:T(8,128)(2,1)S(1)}, u32[]{:S(2)}, u32[]{:S(2)}) collective-permute-start(bf16[128,1024]{1,0:T(8,128)(2,1)S(1)} %slice.1577), channel_id=1, source_target_pairs={{0,2},{1,3},{2,0},{3,1},{4,6},{5,7},{6,4},{7,5},{8,10},{9,11},{10,... | collective-permute-start | bytes 786440 | tf_op jit(solution)/shard_map/ppermute | solution.py:77
  298.3 21.3 %collective-permute-start.21 = (bf16[64,2048]{1,0:T(8,128)(2,1)S(1)}, bf16[64,2048]{1,0:T(8,128)(2,1)S(1)}, u32[]{:S(2)}, u32[]{:S(2)}) collective-permute-start(bf16[64,2048]{1,0:T(8,128)(2,1)S(1)} %fusion.71), channel_id=1, source_target_pairs={{0,4},{1,5},{2,6},{3,7},{4,0},{5,1},{6,2},{7,3},{8,12},{9,13},{10,... | collective-permute-start | bytes 786440 | tf_op jit(solution)/shard_map/ppermute | solution.py:77
  299.9 78.2 %collective-permute-start.27 = (bf16[2048,512]{1,0:T(8,128)(2,1)S(1)}, bf16[2048,512]{1,0:T(8,128)(2,1)}, u32[]{:S(2)}, u32[]{:S(2)}) collective-permute-start(bf16[2048,512]{1,0:T(8,128)(2,1)S(1)} %copy-done.3), channel_id=1, source_target_pairs={{0,16},{16,0},{1,17},{17,1},{2,18},{18,2},{3,19},{19,3},{4,20},{20... | collective-permute-start | bytes 6291464 | tf_op jit(solution)/shard_map/ppermute | solution.py:77
  319.7 58.3 %collective-permute-start.28 = (bf16[2048,512]{1,0:T(8,128)(2,1)}, bf16[2048,512]{1,0:T(8,128)(2,1)}, u32[]{:S(2)}, u32[]{:S(2)}) collective-permute-start(bf16[2048,512]{1,0:T(8,128)(2,1)} %all-gather.15.cloned.1.call-done.refs_2_), channel_id=1, source_target_pairs={{0,16},{16,0},{1,17},{17,1},{2,18},{18,2},{3,19},{19,3},{4,20},{20... | collective-permute-start | bytes 6291464 | tf_op jit(solution)/shard_map/ppermute | solution.py:77
  323.0 118.6 %all-gather.19.cloned.1.call-start = ((), (), s32[]{:S(2)}) async-start(), calls=%async_computation.25 | async-start | bytes 3145728 | tf_op jit(solution)/shard_map/all_gather | solution.py:639
  377.9 18.9 %collective-permute-start.29 = (bf16[2048,512]{1,0:T(8,128)(2,1)}, bf16[2048,512]{1,0:T(8,128)(2,1)}, u32[]{:S(2)}, u32[]{:S(2)}) collective-permute-start(bf16[2048,512]{1,0:T(8,128)(2,1)} %all-gather.17.cloned.1.call-done.refs_0_), channel_id=1, source_target_pairs={{0,16},{16,0},{1,17},{17,1},{2,18},{18,2},{3,19},{19,3},{4,20},{20... | collective-permute-start | bytes 6291464 | tf_op jit(solution)/shard_map/ppermute | solution.py:77
  378.0 115.3 %all-gather.21.cloned.1.call-start = ((), (), s32[]{:S(2)}) async-start(), calls=%async_computation.26 | async-start | bytes 3145728 | tf_op jit(solution)/shard_map/all_gather | solution.py:639
  409.2 14.6 %collective-permute-start.32 = (bf16[256,1024]{1,0:T(8,128)(2,1)S(1)}, bf16[256,1024]{1,0:T(8,128)(2,1)S(1)}, u32[]{:S(2)}, u32[]{:S(2)}) collective-permute-start(bf16[256,1024]{1,0:T(8,128)(2,1)S(1)} %pad_maximum_fusion.30), channel_id=1, source_target_pairs={{0,2},{1,3},{2,0},{3,1},{4,6},{5,7},{6,4},{7,5},{8,10},{9,11},{10,... | collective-permute-start | bytes 1572872 | tf_op jit(solution)/shard_map/ppermute | solution.py:77
  432.1 32.7 %collective-permute-start.41 = (bf16[2048,384]{1,0:T(8,128)(2,1)}, bf16[2048,384]{1,0:T(8,128)(2,1)}, u32[]{:S(2)}, u32[]{:S(2)}) collective-permute-start(bf16[2048,384]{1,0:T(8,128)(2,1)} %all-gather.11.cloned.1.call-done), channel_id=1, source_target_pairs={{0,16},{16,0},{1,17},{17,1},{2,18},{18,2},{3,19},{19,3},{4,20},{20... | collective-permute-start | bytes 4718600 | tf_op jit(solution)/shard_map/ppermute | solution.py:77
  432.2 122.4 %all-gather.23.cloned.1.call-start = ((), (), s32[]{:S(2)}) async-start(), calls=%async_computation.27 | async-start | bytes 3145728 | tf_op jit(solution)/shard_map/all_gather | solution.py:639
  467.1 317.8 %reduce-scatter.9.cloned.1.call-start = ((), (), s32[]{:S(2)}) async-start(), calls=%async_computation.28 | async-start | bytes 3145728 | tf_op jit(solution)/shard_map/reduce_scatter | solution.py:433
  501.3 33.4 %collective-permute-start.40 = (bf16[512,128]{1,0:T(8,128)(2,1)}, bf16[512,128]{1,0:T(8,128)(2,1)S(1)}, u32[]{:S(2)}, u32[]{:S(2)}) collective-permute-start(bf16[512,128]{1,0:T(8,128)(2,1)} %pad_maximum_fusion.70), channel_id=1, source_target_pairs={{0,8},{8,0},{1,9},{9,1},{2,10},{10,2},{3,11},{11,3},{4,12},{12,4},... | collective-permute-start | bytes 393224 | tf_op jit(solution)/shard_map/ppermute | solution.py:77
  579.7 24.8 %collective-permute-start.53 = (bf16[2048,512]{1,0:T(8,128)(2,1)S(1)}, bf16[2048,512]{1,0:T(8,128)(2,1)S(1)}, u32[]{:S(2)}, u32[]{:S(2)}) collective-permute-start(bf16[2048,512]{1,0:T(8,128)(2,1)S(1)} %copy-done.2), channel_id=1, source_target_pairs={{0,16},{16,0},{1,17},{17,1},{2,18},{18,2},{3,19},{19,3},{4,20},{20... | collective-permute-start | bytes 6291464 | tf_op jit(solution)/shard_map/ppermute | solution.py:77
  579.7 24.7 %collective-permute-start.54 = (bf16[2048,512]{1,0:T(8,128)(2,1)S(1)}, bf16[2048,512]{1,0:T(8,128)(2,1)S(1)}, u32[]{:S(2)}, u32[]{:S(2)}) collective-permute-start(bf16[2048,512]{1,0:T(8,128)(2,1)S(1)} %copy-done.92), channel_id=1, source_target_pairs={{0,16},{16,0},{1,17},{17,1},{2,18},{18,2},{3,19},{19,3},{4,20},{20... | collective-permute-start | bytes 6291464 | tf_op jit(solution)/shard_map/ppermute | solution.py:77
  604.4 28.2 %collective-permute-start.42 = (bf16[2048,512]{1,0:T(8,128)(2,1)S(1)}, bf16[2048,512]{1,0:T(8,128)(2,1)}, u32[]{:S(2)}, u32[]{:S(2)}) collective-permute-start(bf16[2048,512]{1,0:T(8,128)(2,1)S(1)} %copy-done), channel_id=1, source_target_pairs={{0,16},{16,0},{1,17},{17,1},{2,18},{18,2},{3,19},{19,3},{4,20},{20... | collective-permute-start | bytes 6291464 | tf_op jit(solution)/shard_map/ppermute | solution.py:77
  679.5 182.0 %reduce-scatter.11.cloned.1.call-start = ((), (), s32[]{:S(2)}) async-start(), calls=%async_computation.29 | async-start | bytes 3145728 | tf_op jit(solution)/shard_map/reduce_scatter | solution.py:433
  682.9 26.1 %collective-permute-start.67 = (bf16[2048,512]{1,0:T(8,128)(2,1)S(1)}, bf16[2048,512]{1,0:T(8,128)(2,1)S(1)}, u32[]{:S(2)}, u32[]{:S(2)}) collective-permute-start(bf16[2048,512]{1,0:T(8,128)(2,1)S(1)} %convolution_convert_fusion.9), channel_id=1, source_target_pairs={{0,16},{16,0},{1,17},{17,1},{2,18},{18,2},{3,19},{19,3},{4,20},{20... | collective-permute-start | bytes 6291464 | tf_op jit(solution)/shard_map/ppermute | solution.py:77
  717.0 48.6 %collective-permute-start.73 = (bf16[2048,512]{1,0:T(8,128)(2,1)}, bf16[2048,512]{1,0:T(8,128)(2,1)}, u32[]{:S(2)}, u32[]{:S(2)}) collective-permute-start(bf16[2048,512]{1,0:T(8,128)(2,1)} %convolution_convert_fusion.8), channel_id=1, source_target_pairs={{0,16},{16,0},{1,17},{17,1},{2,18},{18,2},{3,19},{19,3},{4,20},{20... | collective-permute-start | bytes 6291464 | tf_op jit(solution)/shard_map/ppermute | solution.py:77
  717.0 20.8 %collective-permute-start.68 = (bf16[64,2048]{1,0:T(8,128)(2,1)S(1)}, bf16[64,2048]{1,0:T(8,128)(2,1)S(1)}, u32[]{:S(2)}, u32[]{:S(2)}) collective-permute-start(bf16[64,2048]{1,0:T(8,128)(2,1)S(1)} %fusion.204), channel_id=1, source_target_pairs={{0,4},{1,5},{2,6},{3,7},{4,0},{5,1},{6,2},{7,3},{8,12},{9,13},{10,... | collective-permute-start | bytes 786440 | tf_op jit(solution)/shard_map/ppermute | solution.py:77
  794.5 67.0 %all-to-all-start.4 = ((bf16[4,256,512]{2,1,0:T(8,128)(2,1)}), bf16[4,256,512]{2,1,0:T(8,128)(2,1)}, u32[]{:S(2)}, u32[]{:S(2)}) async-start(bf16[4,256,512]{2,1,0:T(8,128)(2,1)} %bitcast.278), calls=%async_computation.6 | async-start | bytes 2097152 | tf_op jit(solution)/shard_map/all_to_all | solution.py:72
  798.8 95.8 %reduce-scatter.13.cloned.1.call-start = ((), (), s32[]{:S(2)}) async-start(), calls=%async_computation.30 | async-start | bytes 3145728 | tf_op jit(solution)/shard_map/reduce_scatter | solution.py:433
  799.5 167.2 %reduce-scatter.15.cloned.1.call-start = ((), (), s32[]{:S(2)}) async-start(), calls=%async_computation.31 | async-start | bytes 2359296 | tf_op jit(solution)/shard_map/reduce_scatter | solution.py:433
  807.3 17.6 %collective-permute-start.75 = (bf16[256,1024]{1,0:T(8,128)(2,1)}, bf16[256,1024]{1,0:T(8,128)(2,1)}, u32[]{:S(2)}, u32[]{:S(2)}) collective-permute-start(bf16[256,1024]{1,0:T(8,128)(2,1)} %slice.979), channel_id=1, source_target_pairs={{0,1},{1,0},{2,3},{3,2},{4,5},{5,4},{6,7},{7,6},{8,9},{9,8},{10,11... | collective-permute-start | bytes 1572872 | tf_op jit(solution)/shard_map/ppermute | solution.py:77
  812.7 47.2 %collective-permute-start.80 = (bf16[2048,384]{0,1:T(8,128)(2,1)S(1)}, bf16[2048,384]{0,1:T(8,128)(2,1)S(1)}, u32[]{:S(2)}, u32[]{:S(2)}) collective-permute-start(bf16[2048,384]{0,1:T(8,128)(2,1)S(1)} %pad_maximum_fusion.1), channel_id=1, source_target_pairs={{0,16},{16,0},{1,17},{17,1},{2,18},{18,2},{3,19},{19,3},{4,20},{20... | collective-permute-start | bytes 4718600 | tf_op jit(solution)/shard_map/ppermute | solution.py:77
  832.7 27.0 %collective-permute-start.79 = (bf16[64,2048]{1,0:T(8,128)(2,1)S(1)}, bf16[64,2048]{1,0:T(8,128)(2,1)S(1)}, u32[]{:S(2)}, u32[]{:S(2)}) collective-permute-start(bf16[64,2048]{1,0:T(8,128)(2,1)S(1)} %fusion.56), channel_id=1, source_target_pairs={{0,4},{1,5},{2,6},{3,7},{4,0},{5,1},{6,2},{7,3},{8,12},{9,13},{10,... | collective-permute-start | bytes 786440 | tf_op jit(solution)/shard_map/ppermute | solution.py:77
  881.3 148.1 %reduce-scatter.17.cloned.1.call-start = ((), (), s32[]{:S(2)}) async-start(), calls=%async_computation.32 | async-start | bytes 3145728 | tf_op jit(solution)/shard_map/reduce_scatter | solution.py:433
  924.1 38.1 %collective-permute-start.92 = (bf16[2048,512]{1,0:T(8,128)(2,1)}, bf16[2048,512]{1,0:T(8,128)(2,1)}, u32[]{:S(2)}, u32[]{:S(2)}) collective-permute-start(bf16[2048,512]{1,0:T(8,128)(2,1)} %convolution_convert_fusion.5), channel_id=1, source_target_pairs={{0,16},{16,0},{1,17},{17,1},{2,18},{18,2},{3,19},{19,3},{4,20},{20... | collective-permute-start | bytes 6291464 | tf_op jit(solution)/shard_map/ppermute | solution.py:77
  924.1 42.6 %all-to-all-start.5 = ((bf16[4,256,512]{2,1,0:T(8,128)(2,1)}), bf16[4,256,512]{2,1,0:T(8,128)(2,1)}, u32[]{:S(2)}, u32[]{:S(2)}) async-start(bf16[4,256,512]{2,1,0:T(8,128)(2,1)} %bitcast.78), calls=%async_computation.9 | async-start | bytes 2097152 | tf_op jit(solution)/shard_map/all_to_all | solution.py:72
  928.4 123.7 %reduce-scatter.19.cloned.1.call-start = ((), (), s32[]{:S(2)}) async-start(), calls=%async_computation.33 | async-start | bytes 3145728 | tf_op jit(solution)/shard_map/reduce_scatter | solution.py:433
  967.1 17.5 %collective-permute-start.93 = (bf16[64,2048]{1,0:T(8,128)(2,1)S(1)}, bf16[64,2048]{1,0:T(8,128)(2,1)S(1)}, u32[]{:S(2)}, u32[]{:S(2)}) collective-permute-start(bf16[64,2048]{1,0:T(8,128)(2,1)S(1)} %fusion.203), channel_id=1, source_target_pairs={{0,4},{1,5},{2,6},{3,7},{4,0},{5,1},{6,2},{7,3},{8,12},{9,13},{10,... | collective-permute-start | bytes 786440 | tf_op jit(solution)/shard_map/ppermute | solution.py:77
  973.4 45.3 %collective-permute-start.98 = (bf16[2048,512]{1,0:T(8,128)(2,1)}, bf16[2048,512]{1,0:T(8,128)(2,1)}, u32[]{:S(2)}, u32[]{:S(2)}) collective-permute-start(bf16[2048,512]{1,0:T(8,128)(2,1)} %convolution_convert_fusion.4), channel_id=1, source_target_pairs={{0,16},{16,0},{1,17},{17,1},{2,18},{18,2},{3,19},{19,3},{4,20},{20... | collective-permute-start | bytes 6291464 | tf_op jit(solution)/shard_map/ppermute | solution.py:77
  986.8 37.1 %all-to-all-start.6 = ((bf16[4,256,512]{2,1,0:T(8,128)(2,1)}), bf16[4,256,512]{2,1,0:T(8,128)(2,1)S(1)}, u32[]{:S(2)}, u32[]{:S(2)}) async-start(bf16[4,256,512]{2,1,0:T(8,128)(2,1)} %bitcast.276), calls=%async_computation.11 | async-start | bytes 2097152 | tf_op jit(solution)/shard_map/all_to_all | solution.py:72
  997.4 17.4 %collective-permute-start.97 = (bf16[256,1024]{1,0:T(8,128)(2,1)S(1)}, bf16[256,1024]{1,0:T(8,128)(2,1)}, u32[]{:S(2)}, u32[]{:S(2)}) collective-permute-start(bf16[256,1024]{1,0:T(8,128)(2,1)S(1)} %pad_maximum_fusion.46.right_ref), channel_id=1, source_target_pairs={{0,2},{1,3},{2,0},{3,1},{4,6},{5,7},{6,4},{7,5},{8,10},{9,11},{10,... | collective-permute-start | bytes 1572872 | tf_op jit(solution)/shard_map/ppermute | solution.py:77
  1024.8 27.2 %all-to-all-start.7 = ((bf16[4,256,384]{2,1,0:T(8,128)(2,1)}), bf16[4,256,384]{2,1,0:T(8,128)(2,1)}, u32[]{:S(2)}, u32[]{:S(2)}) async-start(bf16[4,256,384]{2,1,0:T(8,128)(2,1)} %bitcast.84), calls=%async_computation.13 | async-start | bytes 1572864 | tf_op jit(solution)/shard_map/all_to_all | solution.py:72
  1029.1 90.0 %reduce-scatter.21.cloned.1.call-start = ((), (), s32[]{:S(2)}) async-start(), calls=%async_computation.34 | async-start | bytes 3145728 | tf_op jit(solution)/shard_map/reduce_scatter | solution.py:433
  1057.5 23.6 %collective-permute-start.100 = (bf16[256,1024]{1,0:T(8,128)(2,1)}, bf16[256,1024]{1,0:T(8,128)(2,1)}, u32[]{:S(2)}, u32[]{:S(2)}) collective-permute-start(bf16[256,1024]{1,0:T(8,128)(2,1)} %slice.1025), channel_id=1, source_target_pairs={{0,1},{1,0},{2,3},{3,2},{4,5},{5,4},{6,7},{7,6},{8,9},{9,8},{10,11... | collective-permute-start | bytes 1572872 | tf_op jit(solution)/shard_map/ppermute | solution.py:77
  1059.6 20.4 %collective-permute-start.102 = (bf16[256,1024]{1,0:T(8,128)(2,1)}, bf16[256,1024]{1,0:T(8,128)(2,1)S(1)}, u32[]{:S(2)}, u32[]{:S(2)}) collective-permute-start(bf16[256,1024]{1,0:T(8,128)(2,1)} %pad_maximum_fusion.48), channel_id=1, source_target_pairs={{0,2},{1,3},{2,0},{3,1},{4,6},{5,7},{6,4},{7,5},{8,10},{9,11},{10,... | collective-permute-start | bytes 1572872 | tf_op jit(solution)/shard_map/ppermute | solution.py:77
  1061.7 30.3 %all-to-all-start.9 = ((bf16[4,256,512]{2,1,0:T(8,128)(2,1)}), bf16[4,256,512]{2,1,0:T(8,128)(2,1)}, u32[]{:S(2)}, u32[]{:S(2)}) async-start(bf16[4,256,512]{2,1,0:T(8,128)(2,1)} %bitcast.279), calls=%async_computation.17 | async-start | bytes 2097152 | tf_op jit(solution)/shard_map/all_to_all | solution.py:72
  1068.2 45.7 %collective-permute-start.105 = (bf16[2048,384]{0,1:T(8,128)(2,1)}, bf16[2048,384]{0,1:T(8,128)(2,1)}, u32[]{:S(2)}, u32[]{:S(2)}) collective-permute-start(bf16[2048,384]{0,1:T(8,128)(2,1)} %pad_maximum_fusion.2), channel_id=1, source_target_pairs={{0,16},{16,0},{1,17},{17,1},{2,18},{18,2},{3,19},{19,3},{4,20},{20... | collective-permute-start | bytes 4718600 | tf_op jit(solution)/shard_map/ppermute | solution.py:77
  1090.3 19.4 %collective-permute-start.104 = (bf16[64,2048]{1,0:T(8,128)(2,1)}, bf16[64,2048]{1,0:T(8,128)(2,1)}, u32[]{:S(2)}, u32[]{:S(2)}) collective-permute-start(bf16[64,2048]{1,0:T(8,128)(2,1)} %fusion.50), channel_id=1, source_target_pairs={{0,4},{1,5},{2,6},{3,7},{4,0},{5,1},{6,2},{7,3},{8,12},{9,13},{10,... | collective-permute-start | bytes 786440 | tf_op jit(solution)/shard_map/ppermute | solution.py:77
  1092.0 27.1 %all-to-all-start.8 = ((bf16[4,256,512]{2,1,0:T(8,128)(2,1)}), bf16[4,256,512]{2,1,0:T(8,128)(2,1)}, u32[]{:S(2)}, u32[]{:S(2)}) async-start(bf16[4,256,512]{2,1,0:T(8,128)(2,1)} %bitcast.277), calls=%async_computation.15 | async-start | bytes 2097152 | tf_op jit(solution)/shard_map/all_to_all | solution.py:72
  1096.2 75.9 %reduce-scatter.23.cloned.1.call-start = ((), (), s32[]{:S(2)}) async-start(), calls=%async_computation.35 | async-start | bytes 2359296 | tf_op jit(solution)/shard_map/reduce_scatter | solution.py:433
  1113.9 37.5 %collective-permute-start.113 = (bf16[4,256,512]{2,1,0:T(8,128)(2,1)}, bf16[4,256,512]{2,1,0:T(8,128)(2,1)}, u32[]{:S(2)}, u32[]{:S(2)}) collective-permute-start(bf16[4,256,512]{2,1,0:T(8,128)(2,1)} %get-tuple-element.348), channel_id=1, source_target_pairs={{0,16},{16,0},{1,17},{17,1},{2,18},{18,2},{3,19},{19,3},{4,20},{20... | collective-permute-start | bytes 3145736 | tf_op jit(solution)/shard_map/ppermute | solution.py:77
  1119.3 25.5 %all-to-all-start.10 = ((bf16[4,256,512]{2,1,0:T(8,128)(2,1)}), bf16[4,256,512]{2,1,0:T(8,128)(2,1)}, u32[]{:S(2)}, u32[]{:S(2)}) async-start(bf16[4,256,512]{2,1,0:T(8,128)(2,1)} %bitcast.104), calls=%async_computation.18 | async-start | bytes 2097152 | tf_op jit(solution)/shard_map/all_to_all | solution.py:72
  1126.8 31.1 %collective-permute-start.112 = (bf16[4,256,512]{2,1,0:T(8,128)(2,1)}, bf16[4,256,512]{2,1,0:T(8,128)(2,1)}, u32[]{:S(2)}, u32[]{:S(2)}) collective-permute-start(bf16[4,256,512]{2,1,0:T(8,128)(2,1)} %get-tuple-element.350), channel_id=1, source_target_pairs={{0,16},{16,0},{1,17},{17,1},{2,18},{18,2},{3,19},{19,3},{4,20},{20... | collective-permute-start | bytes 3145736 | tf_op jit(solution)/shard_map/ppermute | solution.py:77
  1127.3 20.3 %collective-permute-start.108 = (f32[2,1024]{1,0:T(2,128)S(1)}, f32[2,1024]{1,0:T(2,128)S(1)}, u32[]{:S(2)}, u32[]{:S(2)}) collective-permute-start(f32[2,1024]{1,0:T(2,128)S(1)} %slice_bitcast_fusion), channel_id=1, source_target_pairs={{0,8},{8,0},{1,9},{9,1},{2,10},{10,2},{3,11},{11,3},{4,12},{12,4},... | collective-permute-start | bytes 24584 | tf_op jit(solution)/shard_map/ppermute | solution.py:77
  1147.6 17.1 %collective-permute-start.114 = (bf16[4,256,512]{2,1,0:T(8,128)(2,1)}, bf16[4,256,512]{2,1,0:T(8,128)(2,1)S(1)}, u32[]{:S(2)}, u32[]{:S(2)}) collective-permute-start(bf16[4,256,512]{2,1,0:T(8,128)(2,1)} %get-tuple-element.346), channel_id=1, source_target_pairs={{0,16},{16,0},{1,17},{17,1},{2,18},{18,2},{3,19},{19,3},{4,20},{20... | collective-permute-start | bytes 3145736 | tf_op jit(solution)/shard_map/ppermute | solution.py:77
  1147.7 30.3 %collective-permute-start.109 = (f32[2,512]{1,0:T(2,128)S(1)}, f32[2,512]{1,0:T(2,128)S(1)}, u32[]{:S(2)}, u32[]{:S(2)}) collective-permute-start(f32[2,512]{1,0:T(2,128)S(1)} %broadcast_select_fusion.14), channel_id=1, source_target_pairs={{0,4},{1,5},{2,6},{3,7},{4,0},{5,1},{6,2},{7,3},{8,12},{9,13},{10,... | collective-permute-start | bytes 12296 | tf_op jit(solution)/shard_map/ppermute | solution.py:77
  1174.4 15.3 %all-to-all-start.11 = ((bf16[4,256,384]{2,1,0:T(8,128)(2,1)}), bf16[4,256,384]{2,1,0:T(8,128)(2,1)S(1)}, u32[]{:S(2)}, u32[]{:S(2)}) async-start(bf16[4,256,384]{2,1,0:T(8,128)(2,1)} %bitcast.105), calls=%async_computation.19 | async-start | bytes 1572864 | tf_op jit(solution)/shard_map/all_to_all | solution.py:72
  (248 other events, 3217.2 us)
Sparse Core Ops, SparseCore 0:
  55.1 44.2 all-gather.8
  120.9 47.1 all-gather.10
  175.9 56.0 all-gather.12
  259.5 54.8 all-gather.14
  323.1 54.7 all-gather.16
  379.9 55.6 all-gather.18
  437.7 55.5 all-gather.20
  494.8 59.7 all-gather.22
  679.6 54.0 reduce-scatter.8
  735.9 59.6 reduce-scatter.10
  801.8 56.0 reduce-scatter.12
  881.4 43.9 reduce-scatter.14
  927.6 54.3 reduce-scatter.16
  984.2 54.2 reduce-scatter.18
  1050.9 56.7 reduce-scatter.20
  1119.4 44.3 reduce-scatter.22
where the time goes:
time: 1230 us; the launch traced here: 1220 us
  waiting for transfers between devices  612 us (50%)
  starting transfers between devices  172 us (14%)
  matrix products  136 us (11%)
  Pallas kernels  122 us (10%)
  local copies, waits for them, and re-layouts  85.6 us (7%)
  other arithmetic  71.3 us (6%)
  between operations  18.1 us (1%)
    ppermute x116, waiting for transfers between devices, hop(): return lax.ppermute(block, axis, [(i, i ^ step) for i in range(size)])  506 us
    ppermute x116, starting transfers between devices, hop(): return lax.ppermute(block, axis, [(i, i ^ step) for i in range(size)])  120 us
    all_gather x8, waiting for transfers between devices, rows_of(): return lax.all_gather(held[name][layer], 'grp', axis=0, tiled=True)  72.3 us
    dot_general x20, matrix products, mm_tl(): lax.dot_general(left, right, (((0,), (0,)), ((), ())), preferred_element_...  54.8 us
    all_to_all x12, starting transfers between devices, trade(): return lax.all_to_all(blocks, axes, 0, 0, tiled=True)  49.6 us
    dot_general x12, matrix products, mm(): return jnp.dot(left, right, preferred_element_type=F32)  43 us
    dot_general x12, matrix products, mm_t(): lax.dot_general(left, right, (((1,), (1,)), ((), ())), preferred_element_...  38 us
    all_to_all x12, waiting for transfers between devices, trade(): return lax.all_to_all(blocks, axes, 0, 0, tiled=True)  32.9 us
  transfers between devices with their start and end apart: 144, of which 82 were waited for; matrix products, arithmetic and copies ran while one was open for 21% of the time, Pallas kernels for 9%

commit v1 on v0

--- a/solution.py
+++ b/solution.py
@@ -697,7 +697,7 @@
         ],
         [
             (),
-            (("own", "attn", 1),),
+            (),
             (("own", "gate", 0),),
             (("own", "up", 0),),
             (("own", "down", 0),),
@@ -709,7 +709,7 @@
         return (kept[layer][6] + sum_rows(mm_t(hidden, held["down", layer]))).astype(BF)
 
     outs[0] = stages.run(
-        kept[0][-1], lambda h: close(h, 0), [], (("own", "gate", 1),)
+        kept[0][-1], lambda h: close(h, 0), [], (("own", "attn", 1), ("own", "gate", 1))
     )
     kept[1] = layer_forward(
         stages,

time: 1230 us -> 1240 us (level)
  waiting for transfers between devices: 612 us -> 625 us
  transfers between devices with their start and end apart: 144 -> 144, of which waited for: 82 -> 80; matrix products, arithmetic and copies ran while one was open for 21% -> 21% of each run, Pallas kernels for 9% -> 9%
where the time goes in v1:
time: 1240 us; the launch traced here: 1220 us
  waiting for transfers between devices  625 us (50%)
  starting transfers between devices  166 us (13%)
  matrix products  134 us (11%)
  Pallas kernels  122 us (10%)
  local copies, waits for them, and re-layouts  83.4 us (7%)
  other arithmetic  73.6 us (6%)
  between operations  18.1 us (1%)
    ppermute x116, waiting for transfers between devices, hop(): return lax.ppermute(block, axis, [(i, i ^ step) for i in range(size)])  508 us
    ppermute x116, starting transfers between devices, hop(): return lax.ppermute(block, axis, [(i, i ^ step) for i in range(size)])  115 us
    all_gather x8, waiting for transfers between devices, rows_of(): return lax.all_gather(held[name][layer], 'grp', axis=0, tiled=True)  83.8 us
    dot_general x20, matrix products, mm_tl(): lax.dot_general(left, right, (((0,), (0,)), ((), ())), preferred_element_...  54.8 us
    all_to_all x12, starting transfers between devices, trade(): return lax.all_to_all(blocks, axes, 0, 0, tiled=True)  49 us
    dot_general x12, matrix products, mm(): return jnp.dot(left, right, preferred_element_type=F32)  40.9 us
    dot_general x12, matrix products, mm_t(): lax.dot_general(left, right, (((1,), (1,)), ((), ())), preferred_element_...  38 us
    all_to_all x12, waiting for transfers between devices, trade(): return lax.all_to_all(blocks, axes, 0, 0, tiled=True)  32.9 us
  transfers between devices with their start and end apart: 144, of which 80 were waited for; matrix products, arithmetic and copies ran while one was open for 21% of the time, Pallas kernels for 9%

profile of v1, /device:TPU:0, one launch (start us, length us, event | category | flops | bytes accessed | tf_op | source)
XLA Modules:
  0.0 1222.2 jit_solution(118275895545568883)
XLA Ops:
  38.5 15.2 %all-to-all-done = bf16[8,256,384]{2,1,0:T(8,128)(2,1)S(1)} async-done(((bf16[8,256,384]{2,1,0:T(8,128)(2,1)}), bf16[8,256,384]{2,1,0:T(8,128)(2,1)S(1)}, u32[]{:S(2)}, u32[]{:S(2)}) %all-to-all-start) | async-done | bytes 1572896 | tf_op jit(solution)/shard_map/all_to_all | solution.py:72
  68.2 6.9 collective-permute-done.8
  77.1 7.5 collective-permute-done.7.left_came_ref
  90.6 8.9 all-gather.9.cloned.1.call-done
  121.8 14.3 %collective-permute-done.10 = bf16[512,128]{1,0:T(8,128)(2,1)S(1)} collective-permute-done((bf16[512,128]{1,0:T(8,128)(2,1)S(1)}, bf16[512,128]{1,0:T(8,128)(2,1)S(1)}, u32[]{:S(2)}, u32[]{:S(2)}) %collective-permute-start.10) | collective-permute-done | bytes 131104 | tf_op jit(solution)/shard_map/ppermute | solution.py:77
  150.5 40.6 %collective-permute-done.12 = bf16[64,2048]{1,0:T(8,128)(2,1)S(1)} collective-permute-done((bf16[64,2048]{1,0:T(8,128)(2,1)S(1)}, bf16[64,2048]{1,0:T(8,128)(2,1)S(1)}, u32[]{:S(2)}, u32[]{:S(2)}) %collective-permute-start.12) | collective-permute-done | bytes 262176 | tf_op jit(solution)/shard_map/ppermute | solution.py:77
  203.3 7.1 shard_map.187
  228.6 29.9 %collective-permute-done.19 = bf16[256,1024]{1,0:T(8,128)(2,1)S(1)} collective-permute-done((bf16[256,1024]{1,0:T(8,128)(2,1)S(1)}, bf16[256,1024]{1,0:T(8,128)(2,1)S(1)}, u32[]{:S(2)}, u32[]{:S(2)}) %collective-permute-start.19) | collective-permute-done | bytes 524320 | tf_op jit(solution)/shard_map/ppermute | solution.py:77
  260.6 5.9 collective-permute-done.20
  273.0 15.9 %collective-permute-done.21 = bf16[64,2048]{1,0:T(8,128)(2,1)S(1)} collective-permute-done((bf16[64,2048]{1,0:T(8,128)(2,1)S(1)}, bf16[64,2048]{1,0:T(8,128)(2,1)S(1)}, u32[]{:S(2)}, u32[]{:S(2)}) %collective-permute-start.21) | collective-permute-done | bytes 262176 | tf_op jit(solution)/shard_map/ppermute | solution.py:77
  291.2 12.6 %collective-permute-done.22 = bf16[64,2048]{1,0:T(8,128)(2,1)} collective-permute-done((bf16[64,2048]{1,0:T(8,128)(2,1)}, bf16[64,2048]{1,0:T(8,128)(2,1)}, u32[]{:S(2)}, u32[]{:S(2)}) %collective-permute-start.22) | collective-permute-done | bytes 262176 | tf_op jit(solution)/shard_map/ppermute | solution.py:77
  307.3 5.6 collective-permute-done.23
  316.2 10.3 collective-permute-done.24.left_came_ref
  331.6 9.6 all-gather.15.cloned.1.call-done.refs_0_
  341.3 8.3 shard_map.190
  349.6 7.2 fusion.248
  360.0 6.2 shard_map.191
  374.1 11.1 collective-permute-done.30
  395.2 10.1 collective-permute-done.34
  406.1 38.1 %all-gather.19.cloned.1.call-done.refs_0_ = bf16[2048,512]{1,0:T(8,128)(2,1)} async-done(((bf16[1024,512]{1,0:T(8,128)(2,1)}), bf16[2048,512]{1,0:T(8,128)(2,1)}) %all-gather.19.cloned.1.call-update) | async-done | bytes 2097168 | tf_op jit(solution)/shard_map/all_gather | solution.py:639
  444.6 8.0 collective-permute-done.35
  463.6 8.7 collective-permute-done.37.left_came_ref
  477.3 23.9 %all-gather.21.cloned.1.call-done.refs_2_ = bf16[2048,512]{1,0:T(8,128)(2,1)} async-done(((bf16[1024,512]{1,0:T(8,128)(2,1)}), bf16[2048,512]{1,0:T(8,128)(2,1)}) %all-gather.21.cloned.1.call-update) | async-done | bytes 2097168 | tf_op jit(solution)/shard_map/all_gather | solution.py:639
  509.4 29.7 %collective-permute-done.40 = bf16[512,128]{1,0:T(8,128)(2,1)S(1)} collective-permute-done((bf16[512,128]{1,0:T(8,128)(2,1)S(1)}, bf16[512,128]{1,0:T(8,128)(2,1)S(1)}, u32[]{:S(2)}, u32[]{:S(2)}) %collective-permute-start.40) | collective-permute-done | bytes 131104 | tf_op jit(solution)/shard_map/ppermute | solution.py:77
  546.3 7.1 shard_map.193
  565.8 9.5 collective-permute-done.43
  586.1 6.3 collective-permute-done.47
  592.8 6.4 collective-permute-done.48
  600.9 6.7 collective-permute-done.49
  613.2 8.1 shard_map.196
  626.0 7.7 fusion.249
  638.8 6.0 shard_map.194
  647.4 5.0 convolution_convert_fusion
  658.2 8.4 collective-permute-done.58
  668.7 5.5 collective-permute-done.59
  675.5 4.8 convolution_convert_fusion.11
  688.8 5.1 collective-permute-done.62
  704.2 10.6 collective-permute-done.66
  725.4 18.2 %collective-permute-done.68 = bf16[64,2048]{1,0:T(8,128)(2,1)S(1)} collective-permute-done((bf16[64,2048]{1,0:T(8,128)(2,1)S(1)}, bf16[64,2048]{1,0:T(8,128)(2,1)S(1)}, u32[]{:S(2)}, u32[]{:S(2)}) %collective-permute-start.68) | collective-permute-done | bytes 262176 | tf_op jit(solution)/shard_map/ppermute | solution.py:77
  746.7 5.4 collective-permute-done.69
  755.2 10.1 collective-permute-done.70.left_came_ref
  771.4 5.2 add_convert_fusion.5
  781.5 9.3 shard_map.198
  818.7 9.6 collective-permute-done.77
  840.9 24.7 %collective-permute-done.79 = bf16[64,2048]{1,0:T(8,128)(2,1)S(1)} collective-permute-done((bf16[64,2048]{1,0:T(8,128)(2,1)S(1)}, bf16[64,2048]{1,0:T(8,128)(2,1)S(1)}, u32[]{:S(2)}, u32[]{:S(2)}) %collective-permute-start.79) | collective-permute-done | bytes 262176 | tf_op jit(solution)/shard_map/ppermute | solution.py:77
  868.2 6.3 collective-permute-done.81
  877.8 6.2 collective-permute-done.82
  887.2 7.0 collective-permute-done.83.left_came_ref
  904.8 6.9 multiply_convert_fusion
  911.8 7.4 convolution_convert_fusion.7
  947.3 7.1 collective-permute-done.88
  956.0 12.0 collective-permute-done.91
  979.4 11.2 collective-permute-done.93
  1011.6 9.1 collective-permute-done.97.right_came_ref
  1024.6 5.1 add_convert_fusion.1
  1038.0 9.3 shard_map.201
  1074.2 11.9 collective-permute-done.102
  1103.3 12.5 %collective-permute-done.104 = bf16[64,2048]{1,0:T(8,128)(2,1)} collective-permute-done((bf16[64,2048]{1,0:T(8,128)(2,1)}, bf16[64,2048]{1,0:T(8,128)(2,1)}, u32[]{:S(2)}, u32[]{:S(2)}) %collective-permute-start.104) | collective-permute-done | bytes 262176 | tf_op jit(solution)/shard_map/ppermute | solution.py:77
  1135.1 15.7 %all-to-all-done.10 = bf16[4,256,512]{2,1,0:T(8,128)(2,1)} async-done(((bf16[4,256,512]{2,1,0:T(8,128)(2,1)}), bf16[4,256,512]{2,1,0:T(8,128)(2,1)}, u32[]{:S(2)}, u32[]{:S(2)}) %all-to-all-start.10) | async-done | bytes 1048608 | tf_op jit(solution)/shard_map/all_to_all | solution.py:72
  1157.4 6.4 shard_map.203
  1163.9 6.8 shard_map.202
  1171.7 6.4 shard_map.204
  1186.2 9.5 collective-permute-done.110
  1210.3 4.9 shard_map.206
  (965 shorter events, 520.5 us)
Async XLA Ops:
  29.3 24.4 %all-to-all-start = ((bf16[8,256,384]{2,1,0:T(8,128)(2,1)}), bf16[8,256,384]{2,1,0:T(8,128)(2,1)S(1)}, u32[]{:S(2)}, u32[]{:S(2)}) async-start(bf16[8,256,384]{2,1,0:T(8,128)(2,1)} %bitcast.250), calls=%async_computation | async-start | bytes 3145728 | tf_op jit(solution)/shard_map/all_to_all | solution.py:72
  33.2 66.3 %all-gather.9.cloned.1.call-start = ((), (), s32[]{:S(2)}) async-start(), calls=%async_computation.20 | async-start | bytes 2359296 | tf_op jit(solution)/shard_map/all_gather | solution.py:639
  36.5 22.5 %collective-permute-start.5 = (bf16[64,2048]{1,0:T(8,128)(2,1)S(1)}, bf16[64,2048]{1,0:T(8,128)(2,1)S(1)}, u32[]{:S(2)}, u32[]{:S(2)}) collective-permute-start(bf16[64,2048]{1,0:T(8,128)(2,1)S(1)} %fusion.16), channel_id=1, source_target_pairs={{0,4},{1,5},{2,6},{3,7},{4,0},{5,1},{6,2},{7,3},{8,12},{9,13},{10,... | collective-permute-start | bytes 786440 | tf_op jit(solution)/shard_map/ppermute | solution.py:77
  66.9 17.7 %collective-permute-start.7 = (bf16[256,1024]{1,0:T(8,128)(2,1)S(1)}, bf16[256,1024]{1,0:T(8,128)(2,1)S(1)}, u32[]{:S(2)}, u32[]{:S(2)}) collective-permute-start(bf16[256,1024]{1,0:T(8,128)(2,1)S(1)} %pad_maximum_fusion.23.left_ref), channel_id=1, source_target_pairs={{0,1},{1,0},{2,3},{3,2},{4,5},{5,4},{6,7},{7,6},{8,9},{9,8},{10,11... | collective-permute-start | bytes 1572872 | tf_op jit(solution)/shard_map/ppermute | solution.py:77
  105.4 34.9 %all-to-all-start.1 = ((bf16[8,256,512]{2,1,0:T(8,128)(2,1)}), bf16[8,256,512]{2,1,0:T(8,128)(2,1)}, u32[]{:S(2)}, u32[]{:S(2)}) async-start(bf16[8,256,512]{2,1,0:T(8,128)(2,1)} %bitcast.246), calls=%async_computation.1 | async-start | bytes 4194304 | tf_op jit(solution)/shard_map/all_to_all | solution.py:72
  109.8 26.3 %collective-permute-start.11 = (bf16[2048,384]{1,0:T(8,128)(2,1)}, bf16[2048,384]{1,0:T(8,128)(2,1)}, u32[]{:S(2)}, u32[]{:S(2)}) collective-permute-start(bf16[2048,384]{1,0:T(8,128)(2,1)} %all-gather.9.cloned.1.call-done), channel_id=1, source_target_pairs={{0,16},{16,0},{1,17},{17,1},{2,18},{18,2},{3,19},{19,3},{4,20},{20... | collective-permute-start | bytes 4718600 | tf_op jit(solution)/shard_map/ppermute | solution.py:77
  120.8 15.2 %collective-permute-start.10 = (bf16[512,128]{1,0:T(8,128)(2,1)S(1)}, bf16[512,128]{1,0:T(8,128)(2,1)S(1)}, u32[]{:S(2)}, u32[]{:S(2)}) collective-permute-start(bf16[512,128]{1,0:T(8,128)(2,1)S(1)} %pad_maximum_fusion.69), channel_id=1, source_target_pairs={{0,8},{8,0},{1,9},{9,1},{2,10},{10,2},{3,11},{11,3},{4,12},{12,4},... | collective-permute-start | bytes 393224 | tf_op jit(solution)/shard_map/ppermute | solution.py:77
  140.3 77.7 %all-to-all-start.2 = ((bf16[8,256,512]{2,1,0:T(8,128)(2,1)}), bf16[8,256,512]{2,1,0:T(8,128)(2,1)}, u32[]{:S(2)}, u32[]{:S(2)}) async-start(bf16[8,256,512]{2,1,0:T(8,128)(2,1)} %bitcast.31), calls=%async_computation.2 | async-start | bytes 4194304 | tf_op jit(solution)/shard_map/all_to_all | solution.py:72
  144.8 73.2 %all-gather.11.cloned.1.call-start = ((), (), s32[]{:S(2)}) async-start(), calls=%async_computation.21 | async-start | bytes 3145728 | tf_op jit(solution)/shard_map/all_gather | solution.py:639
  148.1 42.9 %collective-permute-start.12 = (bf16[64,2048]{1,0:T(8,128)(2,1)S(1)}, bf16[64,2048]{1,0:T(8,128)(2,1)S(1)}, u32[]{:S(2)}, u32[]{:S(2)}) collective-permute-start(bf16[64,2048]{1,0:T(8,128)(2,1)S(1)} %copy-done.114), channel_id=1, source_target_pairs={{0,4},{1,5},{2,6},{3,7},{4,0},{5,1},{6,2},{7,3},{8,12},{9,13},{10,... | collective-permute-start | bytes 786440 | tf_op jit(solution)/shard_map/ppermute | solution.py:77
  218.0 49.4 %all-to-all-start.3 = ((bf16[8,256,512]{2,1,0:T(8,128)(2,1)}), bf16[8,256,512]{2,1,0:T(8,128)(2,1)S(1)}, u32[]{:S(2)}, u32[]{:S(2)}) async-start(bf16[8,256,512]{2,1,0:T(8,128)(2,1)} %bitcast.50), calls=%async_computation.3 | async-start | bytes 4194304 | tf_op jit(solution)/shard_map/all_to_all | solution.py:72
  221.6 68.5 %all-gather.13.cloned.1.call-start = ((), (), s32[]{:S(2)}) async-start(), calls=%async_computation.22 | async-start | bytes 3145728 | tf_op jit(solution)/shard_map/all_gather | solution.py:639
  224.7 116.5 %all-gather.15.cloned.1.call-start = ((), (), s32[]{:S(2)}) async-start(), calls=%async_computation.23 | async-start | bytes 3145728 | tf_op jit(solution)/shard_map/all_gather | solution.py:639
  226.0 32.5 %collective-permute-start.19 = (bf16[256,1024]{1,0:T(8,128)(2,1)S(1)}, bf16[256,1024]{1,0:T(8,128)(2,1)S(1)}, u32[]{:S(2)}, u32[]{:S(2)}) collective-permute-start(bf16[256,1024]{1,0:T(8,128)(2,1)S(1)} %pad_maximum_fusion.27), channel_id=1, source_target_pairs={{0,2},{1,3},{2,0},{3,1},{4,6},{5,7},{6,4},{7,5},{8,10},{9,11},{10,... | collective-permute-start | bytes 1572872 | tf_op jit(solution)/shard_map/ppermute | solution.py:77
  228.0 31.3 %collective-permute-start.17 = (bf16[256,1024]{1,0:T(8,128)(2,1)S(1)}, bf16[256,1024]{1,0:T(8,128)(2,1)S(1)}, u32[]{:S(2)}, u32[]{:S(2)}) collective-permute-start(bf16[256,1024]{1,0:T(8,128)(2,1)S(1)} %slice.872), channel_id=1, source_target_pairs={{0,1},{1,0},{2,3},{3,2},{4,5},{5,4},{6,7},{7,6},{8,9},{9,8},{10,11... | collective-permute-start | bytes 1572872 | tf_op jit(solution)/shard_map/ppermute | solution.py:77
  269.0 137.1 %all-gather.17.cloned.1.call-start = ((), (), s32[]{:S(2)}) async-start(), calls=%async_computation.24 | async-start | bytes 2359296 | tf_op jit(solution)/shard_map/all_gather | solution.py:639
  271.4 17.6 %collective-permute-start.21 = (bf16[64,2048]{1,0:T(8,128)(2,1)S(1)}, bf16[64,2048]{1,0:T(8,128)(2,1)S(1)}, u32[]{:S(2)}, u32[]{:S(2)}) collective-permute-start(bf16[64,2048]{1,0:T(8,128)(2,1)S(1)} %fusion.71), channel_id=1, source_target_pairs={{0,4},{1,5},{2,6},{3,7},{4,0},{5,1},{6,2},{7,3},{8,12},{9,13},{10,... | collective-permute-start | bytes 786440 | tf_op jit(solution)/shard_map/ppermute | solution.py:77
  273.0 68.3 %collective-permute-start.27 = (bf16[2048,512]{1,0:T(8,128)(2,1)S(1)}, bf16[2048,512]{1,0:T(8,128)(2,1)}, u32[]{:S(2)}, u32[]{:S(2)}) collective-permute-start(bf16[2048,512]{1,0:T(8,128)(2,1)S(1)} %copy-done.3), channel_id=1, source_target_pairs={{0,16},{16,0},{1,17},{17,1},{2,18},{18,2},{3,19},{19,3},{4,20},{20... | collective-permute-start | bytes 6291464 | tf_op jit(solution)/shard_map/ppermute | solution.py:77
  290.1 51.2 %collective-permute-start.28 = (bf16[2048,512]{1,0:T(8,128)(2,1)}, bf16[2048,512]{1,0:T(8,128)(2,1)}, u32[]{:S(2)}, u32[]{:S(2)}) collective-permute-start(bf16[2048,512]{1,0:T(8,128)(2,1)} %all-gather.13.cloned.1.call-done.refs_2_), channel_id=1, source_target_pairs={{0,16},{16,0},{1,17},{17,1},{2,18},{18,2},{3,19},{19,3},{4,20},{20... | collective-permute-start | bytes 6291464 | tf_op jit(solution)/shard_map/ppermute | solution.py:77
  291.2 153.0 %all-gather.19.cloned.1.call-start = ((), (), s32[]{:S(2)}) async-start(), calls=%async_computation.25 | async-start | bytes 3145728 | tf_op jit(solution)/shard_map/all_gather | solution.py:639
  341.2 18.8 %collective-permute-start.29 = (bf16[2048,512]{1,0:T(8,128)(2,1)}, bf16[2048,512]{1,0:T(8,128)(2,1)}, u32[]{:S(2)}, u32[]{:S(2)}) collective-permute-start(bf16[2048,512]{1,0:T(8,128)(2,1)} %all-gather.15.cloned.1.call-done.refs_0_), channel_id=1, source_target_pairs={{0,16},{16,0},{1,17},{17,1},{2,18},{18,2},{3,19},{19,3},{4,20},{20... | collective-permute-start | bytes 6291464 | tf_op jit(solution)/shard_map/ppermute | solution.py:77
  341.2 160.0 %all-gather.21.cloned.1.call-start = ((), (), s32[]{:S(2)}) async-start(), calls=%async_computation.26 | async-start | bytes 3145728 | tf_op jit(solution)/shard_map/all_gather | solution.py:639
  395.2 164.9 %all-gather.23.cloned.1.call-start = ((), (), s32[]{:S(2)}) async-start(), calls=%async_computation.27 | async-start | bytes 3145728 | tf_op jit(solution)/shard_map/all_gather | solution.py:639
  463.1 76.8 %collective-permute-start.41 = (bf16[2048,384]{1,0:T(8,128)(2,1)}, bf16[2048,384]{1,0:T(8,128)(2,1)}, u32[]{:S(2)}, u32[]{:S(2)}) collective-permute-start(bf16[2048,384]{1,0:T(8,128)(2,1)} %all-gather.17.cloned.1.call-done), channel_id=1, source_target_pairs={{0,16},{16,0},{1,17},{17,1},{2,18},{18,2},{3,19},{19,3},{4,20},{20... | collective-permute-start | bytes 4718600 | tf_op jit(solution)/shard_map/ppermute | solution.py:77
  463.1 327.7 %reduce-scatter.9.cloned.1.call-start = ((), (), s32[]{:S(2)}) async-start(), calls=%async_computation.28 | async-start | bytes 3145728 | tf_op jit(solution)/shard_map/reduce_scatter | solution.py:433
  507.1 32.0 %collective-permute-start.40 = (bf16[512,128]{1,0:T(8,128)(2,1)S(1)}, bf16[512,128]{1,0:T(8,128)(2,1)S(1)}, u32[]{:S(2)}, u32[]{:S(2)}) collective-permute-start(bf16[512,128]{1,0:T(8,128)(2,1)S(1)} %pad_maximum_fusion.70), channel_id=1, source_target_pairs={{0,8},{8,0},{1,9},{9,1},{2,10},{10,2},{3,11},{11,3},{4,12},{12,4},... | collective-permute-start | bytes 393224 | tf_op jit(solution)/shard_map/ppermute | solution.py:77
  585.5 25.1 %collective-permute-start.53 = (bf16[2048,512]{1,0:T(8,128)(2,1)S(1)}, bf16[2048,512]{1,0:T(8,128)(2,1)S(1)}, u32[]{:S(2)}, u32[]{:S(2)}) collective-permute-start(bf16[2048,512]{1,0:T(8,128)(2,1)S(1)} %copy-done.2), channel_id=1, source_target_pairs={{0,16},{16,0},{1,17},{17,1},{2,18},{18,2},{3,19},{19,3},{4,20},{20... | collective-permute-start | bytes 6291464 | tf_op jit(solution)/shard_map/ppermute | solution.py:77
  585.6 25.0 %collective-permute-start.54 = (bf16[2048,512]{1,0:T(8,128)(2,1)S(1)}, bf16[2048,512]{1,0:T(8,128)(2,1)S(1)}, u32[]{:S(2)}, u32[]{:S(2)}) collective-permute-start(bf16[2048,512]{1,0:T(8,128)(2,1)S(1)} %copy-done.96), channel_id=1, source_target_pairs={{0,16},{16,0},{1,17},{17,1},{2,18},{18,2},{3,19},{19,3},{4,20},{20... | collective-permute-start | bytes 6291464 | tf_op jit(solution)/shard_map/ppermute | solution.py:77
  610.6 28.2 %collective-permute-start.42 = (bf16[2048,512]{1,0:T(8,128)(2,1)S(1)}, bf16[2048,512]{1,0:T(8,128)(2,1)}, u32[]{:S(2)}, u32[]{:S(2)}) collective-permute-start(bf16[2048,512]{1,0:T(8,128)(2,1)S(1)} %copy-done), channel_id=1, source_target_pairs={{0,16},{16,0},{1,17},{17,1},{2,18},{18,2},{3,19},{19,3},{4,20},{20... | collective-permute-start | bytes 6291464 | tf_op jit(solution)/shard_map/ppermute | solution.py:77
  685.3 182.1 %reduce-scatter.11.cloned.1.call-start = ((), (), s32[]{:S(2)}) async-start(), calls=%async_computation.29 | async-start | bytes 3145728 | tf_op jit(solution)/shard_map/reduce_scatter | solution.py:433
  688.7 26.1 %collective-permute-start.67 = (bf16[2048,512]{1,0:T(8,128)(2,1)S(1)}, bf16[2048,512]{1,0:T(8,128)(2,1)S(1)}, u32[]{:S(2)}, u32[]{:S(2)}) collective-permute-start(bf16[2048,512]{1,0:T(8,128)(2,1)S(1)} %convolution_convert_fusion.9), channel_id=1, source_target_pairs={{0,16},{16,0},{1,17},{17,1},{2,18},{18,2},{3,19},{19,3},{4,20},{20... | collective-permute-start | bytes 6291464 | tf_op jit(solution)/shard_map/ppermute | solution.py:77
  722.8 48.6 %collective-permute-start.73 = (bf16[2048,512]{1,0:T(8,128)(2,1)}, bf16[2048,512]{1,0:T(8,128)(2,1)}, u32[]{:S(2)}, u32[]{:S(2)}) collective-permute-start(bf16[2048,512]{1,0:T(8,128)(2,1)} %convolution_convert_fusion.8), channel_id=1, source_target_pairs={{0,16},{16,0},{1,17},{17,1},{2,18},{18,2},{3,19},{19,3},{4,20},{20... | collective-permute-start | bytes 6291464 | tf_op jit(solution)/shard_map/ppermute | solution.py:77
  722.9 20.8 %collective-permute-start.68 = (bf16[64,2048]{1,0:T(8,128)(2,1)S(1)}, bf16[64,2048]{1,0:T(8,128)(2,1)S(1)}, u32[]{:S(2)}, u32[]{:S(2)}) collective-permute-start(bf16[64,2048]{1,0:T(8,128)(2,1)S(1)} %fusion.204), channel_id=1, source_target_pairs={{0,4},{1,5},{2,6},{3,7},{4,0},{5,1},{6,2},{7,3},{8,12},{9,13},{10,... | collective-permute-start | bytes 786440 | tf_op jit(solution)/shard_map/ppermute | solution.py:77
  790.9 14.6 %collective-permute-start.74 = (bf16[512,128]{1,0:T(8,128)(2,1)S(1)}, bf16[512,128]{1,0:T(8,128)(2,1)S(1)}, u32[]{:S(2)}, u32[]{:S(2)}) collective-permute-start(bf16[512,128]{1,0:T(8,128)(2,1)S(1)} %fusion.160), channel_id=1, source_target_pairs={{0,8},{8,0},{1,9},{9,1},{2,10},{10,2},{3,11},{11,3},{4,12},{12,4},... | collective-permute-start | bytes 393224 | tf_op jit(solution)/shard_map/ppermute | solution.py:77
  800.4 67.0 %all-to-all-start.4 = ((bf16[4,256,512]{2,1,0:T(8,128)(2,1)}), bf16[4,256,512]{2,1,0:T(8,128)(2,1)}, u32[]{:S(2)}, u32[]{:S(2)}) async-start(bf16[4,256,512]{2,1,0:T(8,128)(2,1)} %bitcast.278), calls=%async_computation.6 | async-start | bytes 2097152 | tf_op jit(solution)/shard_map/all_to_all | solution.py:72
  804.7 95.8 %reduce-scatter.13.cloned.1.call-start = ((), (), s32[]{:S(2)}) async-start(), calls=%async_computation.30 | async-start | bytes 3145728 | tf_op jit(solution)/shard_map/reduce_scatter | solution.py:433
  805.4 167.2 %reduce-scatter.15.cloned.1.call-start = ((), (), s32[]{:S(2)}) async-start(), calls=%async_computation.31 | async-start | bytes 2359296 | tf_op jit(solution)/shard_map/reduce_scatter | solution.py:433
  813.2 17.6 %collective-permute-start.75 = (bf16[256,1024]{1,0:T(8,128)(2,1)}, bf16[256,1024]{1,0:T(8,128)(2,1)}, u32[]{:S(2)}, u32[]{:S(2)}) collective-permute-start(bf16[256,1024]{1,0:T(8,128)(2,1)} %slice.979), channel_id=1, source_target_pairs={{0,1},{1,0},{2,3},{3,2},{4,5},{5,4},{6,7},{7,6},{8,9},{9,8},{10,11... | collective-permute-start | bytes 1572872 | tf_op jit(solution)/shard_map/ppermute | solution.py:77
  818.6 47.2 %collective-permute-start.80 = (bf16[2048,384]{0,1:T(8,128)(2,1)S(1)}, bf16[2048,384]{0,1:T(8,128)(2,1)S(1)}, u32[]{:S(2)}, u32[]{:S(2)}) collective-permute-start(bf16[2048,384]{0,1:T(8,128)(2,1)S(1)} %pad_maximum_fusion.1), channel_id=1, source_target_pairs={{0,16},{16,0},{1,17},{17,1},{2,18},{18,2},{3,19},{19,3},{4,20},{20... | collective-permute-start | bytes 4718600 | tf_op jit(solution)/shard_map/ppermute | solution.py:77
  838.6 27.0 %collective-permute-start.79 = (bf16[64,2048]{1,0:T(8,128)(2,1)S(1)}, bf16[64,2048]{1,0:T(8,128)(2,1)S(1)}, u32[]{:S(2)}, u32[]{:S(2)}) collective-permute-start(bf16[64,2048]{1,0:T(8,128)(2,1)S(1)} %fusion.56), channel_id=1, source_target_pairs={{0,4},{1,5},{2,6},{3,7},{4,0},{5,1},{6,2},{7,3},{8,12},{9,13},{10,... | collective-permute-start | bytes 786440 | tf_op jit(solution)/shard_map/ppermute | solution.py:77
  887.2 148.2 %reduce-scatter.17.cloned.1.call-start = ((), (), s32[]{:S(2)}) async-start(), calls=%async_computation.32 | async-start | bytes 3145728 | tf_op jit(solution)/shard_map/reduce_scatter | solution.py:433
  930.0 38.1 %collective-permute-start.92 = (bf16[2048,512]{1,0:T(8,128)(2,1)}, bf16[2048,512]{1,0:T(8,128)(2,1)}, u32[]{:S(2)}, u32[]{:S(2)}) collective-permute-start(bf16[2048,512]{1,0:T(8,128)(2,1)} %convolution_convert_fusion.5), channel_id=1, source_target_pairs={{0,16},{16,0},{1,17},{17,1},{2,18},{18,2},{3,19},{19,3},{4,20},{20... | collective-permute-start | bytes 6291464 | tf_op jit(solution)/shard_map/ppermute | solution.py:77
  930.0 42.6 %all-to-all-start.5 = ((bf16[4,256,512]{2,1,0:T(8,128)(2,1)}), bf16[4,256,512]{2,1,0:T(8,128)(2,1)}, u32[]{:S(2)}, u32[]{:S(2)}) async-start(bf16[4,256,512]{2,1,0:T(8,128)(2,1)} %bitcast.78), calls=%async_computation.9 | async-start | bytes 2097152 | tf_op jit(solution)/shard_map/all_to_all | solution.py:72
  934.3 123.7 %reduce-scatter.19.cloned.1.call-start = ((), (), s32[]{:S(2)}) async-start(), calls=%async_computation.33 | async-start | bytes 3145728 | tf_op jit(solution)/shard_map/reduce_scatter | solution.py:433
  973.1 17.5 %collective-permute-start.93 = (bf16[64,2048]{1,0:T(8,128)(2,1)S(1)}, bf16[64,2048]{1,0:T(8,128)(2,1)S(1)}, u32[]{:S(2)}, u32[]{:S(2)}) collective-permute-start(bf16[64,2048]{1,0:T(8,128)(2,1)S(1)} %fusion.203), channel_id=1, source_target_pairs={{0,4},{1,5},{2,6},{3,7},{4,0},{5,1},{6,2},{7,3},{8,12},{9,13},{10,... | collective-permute-start | bytes 786440 | tf_op jit(solution)/shard_map/ppermute | solution.py:77
  979.3 45.3 %collective-permute-start.98 = (bf16[2048,512]{1,0:T(8,128)(2,1)}, bf16[2048,512]{1,0:T(8,128)(2,1)}, u32[]{:S(2)}, u32[]{:S(2)}) collective-permute-start(bf16[2048,512]{1,0:T(8,128)(2,1)} %convolution_convert_fusion.4), channel_id=1, source_target_pairs={{0,16},{16,0},{1,17},{17,1},{2,18},{18,2},{3,19},{19,3},{4,20},{20... | collective-permute-start | bytes 6291464 | tf_op jit(solution)/shard_map/ppermute | solution.py:77
  992.7 37.1 %all-to-all-start.6 = ((bf16[4,256,512]{2,1,0:T(8,128)(2,1)}), bf16[4,256,512]{2,1,0:T(8,128)(2,1)S(1)}, u32[]{:S(2)}, u32[]{:S(2)}) async-start(bf16[4,256,512]{2,1,0:T(8,128)(2,1)} %bitcast.276), calls=%async_computation.11 | async-start | bytes 2097152 | tf_op jit(solution)/shard_map/all_to_all | solution.py:72
  1003.3 17.5 %collective-permute-start.97 = (bf16[256,1024]{1,0:T(8,128)(2,1)S(1)}, bf16[256,1024]{1,0:T(8,128)(2,1)}, u32[]{:S(2)}, u32[]{:S(2)}) collective-permute-start(bf16[256,1024]{1,0:T(8,128)(2,1)S(1)} %pad_maximum_fusion.46.right_ref), channel_id=1, source_target_pairs={{0,2},{1,3},{2,0},{3,1},{4,6},{5,7},{6,4},{7,5},{8,10},{9,11},{10,... | collective-permute-start | bytes 1572872 | tf_op jit(solution)/shard_map/ppermute | solution.py:77
  1030.8 27.2 %all-to-all-start.7 = ((bf16[4,256,384]{2,1,0:T(8,128)(2,1)}), bf16[4,256,384]{2,1,0:T(8,128)(2,1)}, u32[]{:S(2)}, u32[]{:S(2)}) async-start(bf16[4,256,384]{2,1,0:T(8,128)(2,1)} %bitcast.84), calls=%async_computation.13 | async-start | bytes 1572864 | tf_op jit(solution)/shard_map/all_to_all | solution.py:72
  1035.0 90.0 %reduce-scatter.21.cloned.1.call-start = ((), (), s32[]{:S(2)}) async-start(), calls=%async_computation.34 | async-start | bytes 3145728 | tf_op jit(solution)/shard_map/reduce_scatter | solution.py:433
  1063.4 23.5 %collective-permute-start.100 = (bf16[256,1024]{1,0:T(8,128)(2,1)}, bf16[256,1024]{1,0:T(8,128)(2,1)}, u32[]{:S(2)}, u32[]{:S(2)}) collective-permute-start(bf16[256,1024]{1,0:T(8,128)(2,1)} %slice.1025), channel_id=1, source_target_pairs={{0,1},{1,0},{2,3},{3,2},{4,5},{5,4},{6,7},{7,6},{8,9},{9,8},{10,11... | collective-permute-start | bytes 1572872 | tf_op jit(solution)/shard_map/ppermute | solution.py:77
  1065.7 20.4 %collective-permute-start.102 = (bf16[256,1024]{1,0:T(8,128)(2,1)}, bf16[256,1024]{1,0:T(8,128)(2,1)S(1)}, u32[]{:S(2)}, u32[]{:S(2)}) collective-permute-start(bf16[256,1024]{1,0:T(8,128)(2,1)} %pad_maximum_fusion.48), channel_id=1, source_target_pairs={{0,2},{1,3},{2,0},{3,1},{4,6},{5,7},{6,4},{7,5},{8,10},{9,11},{10,... | collective-permute-start | bytes 1572872 | tf_op jit(solution)/shard_map/ppermute | solution.py:77
  1067.6 30.4 %all-to-all-start.9 = ((bf16[4,256,512]{2,1,0:T(8,128)(2,1)}), bf16[4,256,512]{2,1,0:T(8,128)(2,1)}, u32[]{:S(2)}, u32[]{:S(2)}) async-start(bf16[4,256,512]{2,1,0:T(8,128)(2,1)} %bitcast.279), calls=%async_computation.17 | async-start | bytes 2097152 | tf_op jit(solution)/shard_map/all_to_all | solution.py:72
  1074.2 45.8 %collective-permute-start.105 = (bf16[2048,384]{0,1:T(8,128)(2,1)}, bf16[2048,384]{0,1:T(8,128)(2,1)}, u32[]{:S(2)}, u32[]{:S(2)}) collective-permute-start(bf16[2048,384]{0,1:T(8,128)(2,1)} %pad_maximum_fusion.2), channel_id=1, source_target_pairs={{0,16},{16,0},{1,17},{17,1},{2,18},{18,2},{3,19},{19,3},{4,20},{20... | collective-permute-start | bytes 4718600 | tf_op jit(solution)/shard_map/ppermute | solution.py:77
  1096.3 19.5 %collective-permute-start.104 = (bf16[64,2048]{1,0:T(8,128)(2,1)}, bf16[64,2048]{1,0:T(8,128)(2,1)}, u32[]{:S(2)}, u32[]{:S(2)}) collective-permute-start(bf16[64,2048]{1,0:T(8,128)(2,1)} %fusion.50), channel_id=1, source_target_pairs={{0,4},{1,5},{2,6},{3,7},{4,0},{5,1},{6,2},{7,3},{8,12},{9,13},{10,... | collective-permute-start | bytes 786440 | tf_op jit(solution)/shard_map/ppermute | solution.py:77
  1098.0 27.1 %all-to-all-start.8 = ((bf16[4,256,512]{2,1,0:T(8,128)(2,1)}), bf16[4,256,512]{2,1,0:T(8,128)(2,1)}, u32[]{:S(2)}, u32[]{:S(2)}) async-start(bf16[4,256,512]{2,1,0:T(8,128)(2,1)} %bitcast.277), calls=%async_computation.15 | async-start | bytes 2097152 | tf_op jit(solution)/shard_map/all_to_all | solution.py:72
  1102.2 75.9 %reduce-scatter.23.cloned.1.call-start = ((), (), s32[]{:S(2)}) async-start(), calls=%async_computation.35 | async-start | bytes 2359296 | tf_op jit(solution)/shard_map/reduce_scatter | solution.py:433
  1119.9 37.6 %collective-permute-start.113 = (bf16[4,256,512]{2,1,0:T(8,128)(2,1)}, bf16[4,256,512]{2,1,0:T(8,128)(2,1)}, u32[]{:S(2)}, u32[]{:S(2)}) collective-permute-start(bf16[4,256,512]{2,1,0:T(8,128)(2,1)} %get-tuple-element.348), channel_id=1, source_target_pairs={{0,16},{16,0},{1,17},{17,1},{2,18},{18,2},{3,19},{19,3},{4,20},{20... | collective-permute-start | bytes 3145736 | tf_op jit(solution)/shard_map/ppermute | solution.py:77
  1125.3 25.5 %all-to-all-start.10 = ((bf16[4,256,512]{2,1,0:T(8,128)(2,1)}), bf16[4,256,512]{2,1,0:T(8,128)(2,1)}, u32[]{:S(2)}, u32[]{:S(2)}) async-start(bf16[4,256,512]{2,1,0:T(8,128)(2,1)} %bitcast.104), calls=%async_computation.18 | async-start | bytes 2097152 | tf_op jit(solution)/shard_map/all_to_all | solution.py:72
  1132.8 31.1 %collective-permute-start.112 = (bf16[4,256,512]{2,1,0:T(8,128)(2,1)}, bf16[4,256,512]{2,1,0:T(8,128)(2,1)}, u32[]{:S(2)}, u32[]{:S(2)}) collective-permute-start(bf16[4,256,512]{2,1,0:T(8,128)(2,1)} %get-tuple-element.350), channel_id=1, source_target_pairs={{0,16},{16,0},{1,17},{17,1},{2,18},{18,2},{3,19},{19,3},{4,20},{20... | collective-permute-start | bytes 3145736 | tf_op jit(solution)/shard_map/ppermute | solution.py:77
  1133.3 20.3 %collective-permute-start.108 = (f32[2,1024]{1,0:T(2,128)S(1)}, f32[2,1024]{1,0:T(2,128)S(1)}, u32[]{:S(2)}, u32[]{:S(2)}) collective-permute-start(f32[2,1024]{1,0:T(2,128)S(1)} %slice_bitcast_fusion), channel_id=1, source_target_pairs={{0,8},{8,0},{1,9},{9,1},{2,10},{10,2},{3,11},{11,3},{4,12},{12,4},... | collective-permute-start | bytes 24584 | tf_op jit(solution)/shard_map/ppermute | solution.py:77
  1153.6 17.1 %collective-permute-start.114 = (bf16[4,256,512]{2,1,0:T(8,128)(2,1)}, bf16[4,256,512]{2,1,0:T(8,128)(2,1)S(1)}, u32[]{:S(2)}, u32[]{:S(2)}) collective-permute-start(bf16[4,256,512]{2,1,0:T(8,128)(2,1)} %get-tuple-element.346), channel_id=1, source_target_pairs={{0,16},{16,0},{1,17},{17,1},{2,18},{18,2},{3,19},{19,3},{4,20},{20... | collective-permute-start | bytes 3145736 | tf_op jit(solution)/shard_map/ppermute | solution.py:77
  1153.7 30.3 %collective-permute-start.109 = (f32[2,512]{1,0:T(2,128)S(1)}, f32[2,512]{1,0:T(2,128)S(1)}, u32[]{:S(2)}, u32[]{:S(2)}) collective-permute-start(f32[2,512]{1,0:T(2,128)S(1)} %broadcast_select_fusion.14), channel_id=1, source_target_pairs={{0,4},{1,5},{2,6},{3,7},{4,0},{5,1},{6,2},{7,3},{8,12},{9,13},{10,... | collective-permute-start | bytes 12296 | tf_op jit(solution)/shard_map/ppermute | solution.py:77
  1180.4 15.3 %all-to-all-start.11 = ((bf16[4,256,384]{2,1,0:T(8,128)(2,1)}), bf16[4,256,384]{2,1,0:T(8,128)(2,1)S(1)}, u32[]{:S(2)}, u32[]{:S(2)}) async-start(bf16[4,256,384]{2,1,0:T(8,128)(2,1)} %bitcast.105), calls=%async_computation.19 | async-start | bytes 1572864 | tf_op jit(solution)/shard_map/all_to_all | solution.py:72
  (254 other events, 3243.1 us)
Sparse Core Ops, SparseCore 0:
  55.1 44.2 all-gather.8
  148.2 58.8 all-gather.10
  224.8 58.8 all-gather.12
  285.6 55.5 all-gather.14
  342.6 43.9 all-gather.16
  388.6 55.5 all-gather.18
  445.7 55.4 all-gather.20
  502.8 57.2 all-gather.22
  685.5 54.0 reduce-scatter.8
  741.7 59.5 reduce-scatter.10
  807.8 56.0 reduce-scatter.12
  887.3 43.9 reduce-scatter.14
  933.5 54.2 reduce-scatter.16
  990.1 54.3 reduce-scatter.18
  1056.9 56.6 reduce-scatter.20
  1125.4 44.3 reduce-scatter.22

commit v2 on v0

--- a/solution.py
+++ b/solution.py
@@ -764,10 +764,10 @@
             [group_sum("down", 1), grad_of("gate", 1)],
             [group_sum("gate", 1), grad_of("up", 1)],
             [group_sum("up", 1)],
-            [home("down", 1)],
+            [],
             lambda pair: [attn_grad(1)(pair)],
         ),
-        [(), (), (), (), (), (("sum", "gate", 1), ("home", "down", 1))],
+        [(), (), (), (), (), (("sum", "gate", 1),)],
     )
     grads_in[1] = grad_in.astype(BF)
     grad_mlp = stages.run(grads_in[1], gather_rows, [group_sum("attn", 1)], (("sum", "up", 1),))
@@ -781,7 +781,7 @@
         kept[0],
         lambda h: (),
         (
-            [grad_of("down", 0), home("gate", 1)],
+            [grad_of("down", 0), home("down", 1), home("gate", 1)],
             [group_sum("down", 0), grad_of("gate", 0), home("up", 1)],
             [group_sum("gate", 0), grad_of("up", 0), home("attn", 1)],
             [group_sum("up", 0)],
@@ -790,7 +790,7 @@
         ),
         [
             (),
-            (("sum", "attn", 1), ("home", "gate", 1)),
+            (("sum", "attn", 1), ("home", "down", 1), ("home", "gate", 1)),
             (("sum", "down", 0), ("home", "up", 1)),
             (),
             (("sum", "gate", 0), ("home", "attn", 1)),

time: 1230 us -> 1240 us (level)
  waiting for transfers between devices: 612 us -> 626 us
    ppermute x116, waiting for transfers between devices: 506 us -> 519 us  [hop(): return lax.ppermute(block, axis, [(i, i ^ step) for i in range(size)])]
  transfers between devices with their start and end apart: 144 -> 144, of which waited for: 82 -> 84; matrix products, arithmetic and copies ran while one was open for 21% -> 20% of each run, Pallas kernels for 9% -> 9%
where the time goes in v2:
time: 1240 us; the launch traced here: 1230 us
  waiting for transfers between devices  626 us (50%)
  starting transfers between devices  176 us (14%)
  matrix products  134 us (11%)
  Pallas kernels  122 us (10%)
  local copies, waits for them, and re-layouts  83.1 us (7%)
  other arithmetic  68.9 us (6%)
  between operations  18.1 us (1%)
    ppermute x116, waiting for transfers between devices, hop(): return lax.ppermute(block, axis, [(i, i ^ step) for i in range(size)])  519 us
    ppermute x116, starting transfers between devices, hop(): return lax.ppermute(block, axis, [(i, i ^ step) for i in range(size)])  124 us
    all_gather x8, waiting for transfers between devices, rows_of(): return lax.all_gather(held[name][layer], 'grp', axis=0, tiled=True)  72.2 us
    dot_general x20, matrix products, mm_tl(): lax.dot_general(left, right, (((0,), (0,)), ((), ())), preferred_element_...  51.8 us
    all_to_all x12, starting transfers between devices, trade(): return lax.all_to_all(blocks, axes, 0, 0, tiled=True)  50.2 us
    dot_general x12, matrix products, mm(): return jnp.dot(left, right, preferred_element_type=F32)  42.7 us
    dot_general x12, matrix products, mm_t(): lax.dot_general(left, right, (((1,), (1,)), ((), ())), preferred_element_...  39.8 us
    all_to_all x12, waiting for transfers between devices, trade(): return lax.all_to_all(blocks, axes, 0, 0, tiled=True)  33.5 us
  transfers between devices with their start and end apart: 144, of which 84 were waited for; matrix products, arithmetic and copies ran while one was open for 20% of the time, Pallas kernels for 9%

profile of v2, /device:TPU:0, one launch (start us, length us, event | category | flops | bytes accessed | tf_op | source)
XLA Modules:
  0.0 1228.3 jit_solution(3840237426996915695)
XLA Ops:
  38.5 15.2 %all-to-all-done = bf16[8,256,384]{2,1,0:T(8,128)(2,1)S(1)} async-done(((bf16[8,256,384]{2,1,0:T(8,128)(2,1)}), bf16[8,256,384]{2,1,0:T(8,128)(2,1)S(1)}, u32[]{:S(2)}, u32[]{:S(2)}) %all-to-all-start) | async-done | bytes 1572896 | tf_op jit(solution)/shard_map/all_to_all | solution.py:72
  68.2 6.9 collective-permute-done.8
  77.2 7.5 collective-permute-done.7.left_came_ref
  90.6 8.9 all-gather.9.cloned.1.call-done
  123.1 21.0 %collective-permute-done.10 = bf16[512,128]{1,0:T(8,128)(2,1)S(1)} collective-permute-done((bf16[512,128]{1,0:T(8,128)(2,1)S(1)}, bf16[512,128]{1,0:T(8,128)(2,1)S(1)}, u32[]{:S(2)}, u32[]{:S(2)}) %collective-permute-start.10) | collective-permute-done | bytes 131104 | tf_op jit(solution)/shard_map/ppermute | solution.py:77
  148.3 19.7 %all-gather.11.cloned.1.call-done = bf16[2048,384]{1,0:T(8,128)(2,1)} async-done(((bf16[1024,384]{1,0:T(8,128)(2,1)}), bf16[2048,384]{1,0:T(8,128)(2,1)}) %all-gather.11.cloned.1.call-update) | async-done | bytes 1572880 | tf_op jit(solution)/shard_map/all_gather | solution.py:639
  178.1 41.8 %collective-permute-done.12 = bf16[64,2048]{1,0:T(8,128)(2,1)S(1)} collective-permute-done((bf16[64,2048]{1,0:T(8,128)(2,1)S(1)}, bf16[64,2048]{1,0:T(8,128)(2,1)S(1)}, u32[]{:S(2)}, u32[]{:S(2)}) %collective-permute-start.12) | collective-permute-done | bytes 262176 | tf_op jit(solution)/shard_map/ppermute | solution.py:77
  232.7 7.1 shard_map.187
  259.5 8.1 collective-permute-done.17
  270.6 18.9 %collective-permute-done.19 = bf16[256,1024]{1,0:T(8,128)(2,1)S(1)} collective-permute-done((bf16[256,1024]{1,0:T(8,128)(2,1)}, bf16[256,1024]{1,0:T(8,128)(2,1)S(1)}, u32[]{:S(2)}, u32[]{:S(2)}) %collective-permute-start.19) | collective-permute-done | bytes 524320 | tf_op jit(solution)/shard_map/ppermute | solution.py:77
  299.9 19.8 %collective-permute-done.21 = bf16[64,2048]{1,0:T(8,128)(2,1)S(1)} collective-permute-done((bf16[64,2048]{1,0:T(8,128)(2,1)S(1)}, bf16[64,2048]{1,0:T(8,128)(2,1)S(1)}, u32[]{:S(2)}, u32[]{:S(2)}) %collective-permute-start.21) | collective-permute-done | bytes 262176 | tf_op jit(solution)/shard_map/ppermute | solution.py:77
  323.3 8.7 collective-permute-done.22
  335.1 5.0 collective-permute-done.23
  344.0 9.7 collective-permute-done.24.left_came_ref
  359.0 19.1 %all-gather.17.cloned.1.call-done.refs_0_ = bf16[2048,512]{1,0:T(8,128)(2,1)} async-done(((bf16[1024,512]{1,0:T(8,128)(2,1)}), bf16[2048,512]{1,0:T(8,128)(2,1)}) %all-gather.17.cloned.1.call-update) | async-done | bytes 2097168 | tf_op jit(solution)/shard_map/all_gather | solution.py:639
  378.1 8.3 shard_map.190
  386.5 7.3 fusion.248
  396.9 6.2 shard_map.191
  410.9 11.3 collective-permute-done.30
  432.4 8.5 collective-permute-done.34
  442.1 9.2 collective-permute-done.35
  477.1 16.2 %all-gather.21.cloned.1.call-done.refs_2_ = bf16[2048,512]{1,0:T(8,128)(2,1)} async-done(((bf16[1024,512]{1,0:T(8,128)(2,1)}), bf16[2048,512]{1,0:T(8,128)(2,1)}) %all-gather.21.cloned.1.call-update) | async-done | bytes 2097168 | tf_op jit(solution)/shard_map/all_gather | solution.py:639
  506.4 28.4 %collective-permute-done.40 = bf16[512,128]{1,0:T(8,128)(2,1)S(1)} collective-permute-done((bf16[512,128]{1,0:T(8,128)(2,1)}, bf16[512,128]{1,0:T(8,128)(2,1)S(1)}, u32[]{:S(2)}, u32[]{:S(2)}) %collective-permute-start.40) | collective-permute-done | bytes 131104 | tf_op jit(solution)/shard_map/ppermute | solution.py:77
  535.9 7.1 shard_map.193
  546.5 8.2 all-gather.23.cloned.1.call-done.refs_0_
  560.0 9.8 collective-permute-done.43
  580.3 6.0 collective-permute-done.47
  586.8 6.4 collective-permute-done.48
  595.1 6.1 collective-permute-done.49
  607.2 8.1 shard_map.196
  620.0 7.7 fusion.249
  632.7 6.0 shard_map.194
  641.3 5.0 convolution_convert_fusion
  652.5 8.0 collective-permute-done.58
  663.0 5.1 collective-permute-done.59
  669.8 5.0 convolution_convert_fusion.11
  681.0 7.4 collective-permute-done.62
  697.7 5.6 collective-permute-done.66
  712.2 12.8 %collective-permute-done.68 = bf16[64,2048]{1,0:T(8,128)(2,1)S(1)} collective-permute-done((bf16[64,2048]{1,0:T(8,128)(2,1)S(1)}, bf16[64,2048]{1,0:T(8,128)(2,1)S(1)}, u32[]{:S(2)}, u32[]{:S(2)}) %collective-permute-start.68) | collective-permute-done | bytes 262176 | tf_op jit(solution)/shard_map/ppermute | solution.py:77
  728.6 6.0 collective-permute-done.69
  737.2 10.3 collective-permute-done.70.left_came_ref
  760.6 9.7 shard_map.198
  775.8 28.0 %collective-permute-done.74 = bf16[512,128]{1,0:T(8,128)(2,1)S(1)} collective-permute-done((bf16[512,128]{1,0:T(8,128)(2,1)S(1)}, bf16[512,128]{1,0:T(8,128)(2,1)S(1)}, u32[]{:S(2)}, u32[]{:S(2)}) %collective-permute-start.74) | collective-permute-done | bytes 131104 | tf_op jit(solution)/shard_map/ppermute | solution.py:77
  814.1 8.8 collective-permute-done.75
  834.3 10.6 collective-permute-done.79
  849.9 11.0 collective-permute-done.81
  862.5 6.0 collective-permute-done.82
  872.3 7.2 collective-permute-done.83.left_came_ref
  893.1 6.9 multiply_convert_fusion
  900.1 9.9 convolution_convert_fusion.7
  924.2 6.3 collective-permute-done.89
  933.5 5.0 collective-permute-done.90
  946.4 36.5 %collective-permute-done.91 = bf16[64,2048]{1,0:T(8,128)(2,1)S(1)} collective-permute-done((bf16[64,2048]{1,0:T(8,128)(2,1)S(1)}, bf16[64,2048]{1,0:T(8,128)(2,1)S(1)}, u32[]{:S(2)}, u32[]{:S(2)}) %collective-permute-start.91) | collective-permute-done | bytes 262176 | tf_op jit(solution)/shard_map/ppermute | solution.py:77
  1003.1 6.2 collective-permute-start.95
  1018.5 7.3 collective-permute-done.97.right_came_ref
  1029.7 5.1 add_convert_fusion.1
  1043.1 9.3 shard_map.201
  1081.8 11.4 collective-permute-done.102
  1110.4 10.8 collective-permute-done.104
  1139.8 16.7 %all-to-all-done.10 = bf16[4,256,512]{2,1,0:T(8,128)(2,1)} async-done(((bf16[4,256,512]{2,1,0:T(8,128)(2,1)}), bf16[4,256,512]{2,1,0:T(8,128)(2,1)}, u32[]{:S(2)}, u32[]{:S(2)}) %all-to-all-start.10) | async-done | bytes 1048608 | tf_op jit(solution)/shard_map/all_to_all | solution.py:72
  1163.5 6.4 shard_map.203
  1170.9 6.8 shard_map.202
  1177.7 6.4 shard_map.204
  1192.3 9.5 collective-permute-done.110
  (946 shorter events, 524.9 us)
Async XLA Ops:
  29.3 24.4 %all-to-all-start = ((bf16[8,256,384]{2,1,0:T(8,128)(2,1)}), bf16[8,256,384]{2,1,0:T(8,128)(2,1)S(1)}, u32[]{:S(2)}, u32[]{:S(2)}) async-start(bf16[8,256,384]{2,1,0:T(8,128)(2,1)} %bitcast.248), calls=%async_computation | async-start | bytes 3145728 | tf_op jit(solution)/shard_map/all_to_all | solution.py:72
  33.2 66.3 %all-gather.9.cloned.1.call-start = ((), (), s32[]{:S(2)}) async-start(), calls=%async_computation.20 | async-start | bytes 2359296 | tf_op jit(solution)/shard_map/all_gather | solution.py:639
  36.5 22.5 %collective-permute-start.5 = (bf16[64,2048]{1,0:T(8,128)(2,1)S(1)}, bf16[64,2048]{1,0:T(8,128)(2,1)S(1)}, u32[]{:S(2)}, u32[]{:S(2)}) collective-permute-start(bf16[64,2048]{1,0:T(8,128)(2,1)S(1)} %fusion.16), channel_id=1, source_target_pairs={{0,4},{1,5},{2,6},{3,7},{4,0},{5,1},{6,2},{7,3},{8,12},{9,13},{10,... | collective-permute-start | bytes 786440 | tf_op jit(solution)/shard_map/ppermute | solution.py:77
  66.9 17.7 %collective-permute-start.7 = (bf16[256,1024]{1,0:T(8,128)(2,1)S(1)}, bf16[256,1024]{1,0:T(8,128)(2,1)S(1)}, u32[]{:S(2)}, u32[]{:S(2)}) collective-permute-start(bf16[256,1024]{1,0:T(8,128)(2,1)S(1)} %pad_maximum_fusion.23.left_ref), channel_id=1, source_target_pairs={{0,1},{1,0},{2,3},{3,2},{4,5},{5,4},{6,7},{7,6},{8,9},{9,8},{10,11... | collective-permute-start | bytes 1572872 | tf_op jit(solution)/shard_map/ppermute | solution.py:77
  105.4 62.7 %all-to-all-start.1 = ((bf16[8,256,512]{2,1,0:T(8,128)(2,1)}), bf16[8,256,512]{2,1,0:T(8,128)(2,1)}, u32[]{:S(2)}, u32[]{:S(2)}) async-start(bf16[8,256,512]{2,1,0:T(8,128)(2,1)} %bitcast.244), calls=%async_computation.1 | async-start | bytes 4194304 | tf_op jit(solution)/shard_map/all_to_all | solution.py:72
  109.8 58.3 %all-gather.11.cloned.1.call-start = ((), (), s32[]{:S(2)}) async-start(), calls=%async_computation.21 | async-start | bytes 2359296 | tf_op jit(solution)/shard_map/all_gather | solution.py:639
  109.8 34.3 %collective-permute-start.11 = (bf16[2048,384]{1,0:T(8,128)(2,1)}, bf16[2048,384]{1,0:T(8,128)(2,1)}, u32[]{:S(2)}, u32[]{:S(2)}) collective-permute-start(bf16[2048,384]{1,0:T(8,128)(2,1)} %all-gather.9.cloned.1.call-done), channel_id=1, source_target_pairs={{0,16},{16,0},{1,17},{17,1},{2,18},{18,2},{3,19},{19,3},{4,20},{20... | collective-permute-start | bytes 4718600 | tf_op jit(solution)/shard_map/ppermute | solution.py:77
  120.8 23.3 %collective-permute-start.10 = (bf16[512,128]{1,0:T(8,128)(2,1)S(1)}, bf16[512,128]{1,0:T(8,128)(2,1)S(1)}, u32[]{:S(2)}, u32[]{:S(2)}) collective-permute-start(bf16[512,128]{1,0:T(8,128)(2,1)S(1)} %pad_maximum_fusion.69), channel_id=1, source_target_pairs={{0,8},{8,0},{1,9},{9,1},{2,10},{10,2},{3,11},{11,3},{4,12},{12,4},... | collective-permute-start | bytes 393224 | tf_op jit(solution)/shard_map/ppermute | solution.py:77
  168.1 79.8 %all-to-all-start.2 = ((bf16[8,256,512]{2,1,0:T(8,128)(2,1)}), bf16[8,256,512]{2,1,0:T(8,128)(2,1)}, u32[]{:S(2)}, u32[]{:S(2)}) async-start(bf16[8,256,512]{2,1,0:T(8,128)(2,1)} %bitcast.32), calls=%async_computation.2 | async-start | bytes 4194304 | tf_op jit(solution)/shard_map/all_to_all | solution.py:72
  172.5 75.3 %all-gather.13.cloned.1.call-start = ((), (), s32[]{:S(2)}) async-start(), calls=%async_computation.22 | async-start | bytes 3145728 | tf_op jit(solution)/shard_map/all_gather | solution.py:639
  175.8 44.1 %collective-permute-start.12 = (bf16[64,2048]{1,0:T(8,128)(2,1)S(1)}, bf16[64,2048]{1,0:T(8,128)(2,1)S(1)}, u32[]{:S(2)}, u32[]{:S(2)}) collective-permute-start(bf16[64,2048]{1,0:T(8,128)(2,1)S(1)} %copy-done.108), channel_id=1, source_target_pairs={{0,4},{1,5},{2,6},{3,7},{4,0},{5,1},{6,2},{7,3},{8,12},{9,13},{10,... | collective-permute-start | bytes 786440 | tf_op jit(solution)/shard_map/ppermute | solution.py:77
  247.9 72.2 %all-to-all-start.3 = ((bf16[8,256,512]{2,1,0:T(8,128)(2,1)}), bf16[8,256,512]{2,1,0:T(8,128)(2,1)}, u32[]{:S(2)}, u32[]{:S(2)}) async-start(bf16[8,256,512]{2,1,0:T(8,128)(2,1)} %bitcast.51), calls=%async_computation.3 | async-start | bytes 4194304 | tf_op jit(solution)/shard_map/all_to_all | solution.py:72
  252.2 67.6 %all-gather.15.cloned.1.call-start = ((), (), s32[]{:S(2)}) async-start(), calls=%async_computation.23 | async-start | bytes 3145728 | tf_op jit(solution)/shard_map/all_gather | solution.py:639
  254.6 34.9 %collective-permute-start.19 = (bf16[256,1024]{1,0:T(8,128)(2,1)}, bf16[256,1024]{1,0:T(8,128)(2,1)S(1)}, u32[]{:S(2)}, u32[]{:S(2)}) collective-permute-start(bf16[256,1024]{1,0:T(8,128)(2,1)} %pad_maximum_fusion.27), channel_id=1, source_target_pairs={{0,2},{1,3},{2,0},{3,1},{4,6},{5,7},{6,4},{7,5},{8,10},{9,11},{10,... | collective-permute-start | bytes 1572872 | tf_op jit(solution)/shard_map/ppermute | solution.py:77
  259.5 118.6 %all-gather.17.cloned.1.call-start = ((), (), s32[]{:S(2)}) async-start(), calls=%async_computation.24 | async-start | bytes 3145728 | tf_op jit(solution)/shard_map/all_gather | solution.py:639
  268.9 25.8 %collective-permute-start.18 = (bf16[128,1024]{1,0:T(8,128)(2,1)S(1)}, bf16[128,1024]{1,0:T(8,128)(2,1)S(1)}, u32[]{:S(2)}, u32[]{:S(2)}) collective-permute-start(bf16[128,1024]{1,0:T(8,128)(2,1)S(1)} %slice.1577), channel_id=1, source_target_pairs={{0,2},{1,3},{2,0},{3,1},{4,6},{5,7},{6,4},{7,5},{8,10},{9,11},{10,... | collective-permute-start | bytes 786440 | tf_op jit(solution)/shard_map/ppermute | solution.py:77
  298.4 21.3 %collective-permute-start.21 = (bf16[64,2048]{1,0:T(8,128)(2,1)S(1)}, bf16[64,2048]{1,0:T(8,128)(2,1)S(1)}, u32[]{:S(2)}, u32[]{:S(2)}) collective-permute-start(bf16[64,2048]{1,0:T(8,128)(2,1)S(1)} %fusion.71), channel_id=1, source_target_pairs={{0,4},{1,5},{2,6},{3,7},{4,0},{5,1},{6,2},{7,3},{8,12},{9,13},{10,... | collective-permute-start | bytes 786440 | tf_op jit(solution)/shard_map/ppermute | solution.py:77
  299.9 78.2 %collective-permute-start.27 = (bf16[2048,512]{1,0:T(8,128)(2,1)S(1)}, bf16[2048,512]{1,0:T(8,128)(2,1)}, u32[]{:S(2)}, u32[]{:S(2)}) collective-permute-start(bf16[2048,512]{1,0:T(8,128)(2,1)S(1)} %copy-done.3), channel_id=1, source_target_pairs={{0,16},{16,0},{1,17},{17,1},{2,18},{18,2},{3,19},{19,3},{4,20},{20... | collective-permute-start | bytes 6291464 | tf_op jit(solution)/shard_map/ppermute | solution.py:77
  319.8 58.3 %collective-permute-start.28 = (bf16[2048,512]{1,0:T(8,128)(2,1)}, bf16[2048,512]{1,0:T(8,128)(2,1)}, u32[]{:S(2)}, u32[]{:S(2)}) collective-permute-start(bf16[2048,512]{1,0:T(8,128)(2,1)} %all-gather.15.cloned.1.call-done.refs_2_), channel_id=1, source_target_pairs={{0,16},{16,0},{1,17},{17,1},{2,18},{18,2},{3,19},{19,3},{4,20},{20... | collective-permute-start | bytes 6291464 | tf_op jit(solution)/shard_map/ppermute | solution.py:77
  323.1 118.6 %all-gather.19.cloned.1.call-start = ((), (), s32[]{:S(2)}) async-start(), calls=%async_computation.25 | async-start | bytes 3145728 | tf_op jit(solution)/shard_map/all_gather | solution.py:639
  378.0 18.9 %collective-permute-start.29 = (bf16[2048,512]{1,0:T(8,128)(2,1)}, bf16[2048,512]{1,0:T(8,128)(2,1)}, u32[]{:S(2)}, u32[]{:S(2)}) collective-permute-start(bf16[2048,512]{1,0:T(8,128)(2,1)} %all-gather.17.cloned.1.call-done.refs_0_), channel_id=1, source_target_pairs={{0,16},{16,0},{1,17},{17,1},{2,18},{18,2},{3,19},{19,3},{4,20},{20... | collective-permute-start | bytes 6291464 | tf_op jit(solution)/shard_map/ppermute | solution.py:77
  378.1 115.3 %all-gather.21.cloned.1.call-start = ((), (), s32[]{:S(2)}) async-start(), calls=%async_computation.26 | async-start | bytes 3145728 | tf_op jit(solution)/shard_map/all_gather | solution.py:639
  409.4 14.6 %collective-permute-start.32 = (bf16[256,1024]{1,0:T(8,128)(2,1)S(1)}, bf16[256,1024]{1,0:T(8,128)(2,1)S(1)}, u32[]{:S(2)}, u32[]{:S(2)}) collective-permute-start(bf16[256,1024]{1,0:T(8,128)(2,1)S(1)} %pad_maximum_fusion.30), channel_id=1, source_target_pairs={{0,2},{1,3},{2,0},{3,1},{4,6},{5,7},{6,4},{7,5},{8,10},{9,11},{10,... | collective-permute-start | bytes 1572872 | tf_op jit(solution)/shard_map/ppermute | solution.py:77
  432.2 32.7 %collective-permute-start.41 = (bf16[2048,384]{1,0:T(8,128)(2,1)}, bf16[2048,384]{1,0:T(8,128)(2,1)}, u32[]{:S(2)}, u32[]{:S(2)}) collective-permute-start(bf16[2048,384]{1,0:T(8,128)(2,1)} %all-gather.11.cloned.1.call-done), channel_id=1, source_target_pairs={{0,16},{16,0},{1,17},{17,1},{2,18},{18,2},{3,19},{19,3},{4,20},{20... | collective-permute-start | bytes 4718600 | tf_op jit(solution)/shard_map/ppermute | solution.py:77
  432.3 122.3 %all-gather.23.cloned.1.call-start = ((), (), s32[]{:S(2)}) async-start(), calls=%async_computation.27 | async-start | bytes 3145728 | tf_op jit(solution)/shard_map/all_gather | solution.py:639
  467.3 379.3 %reduce-scatter.9.cloned.1.call-start = ((), (), s32[]{:S(2)}) async-start(), calls=%async_computation.28 | async-start | bytes 3145728 | tf_op jit(solution)/shard_map/reduce_scatter | solution.py:433
  501.4 33.4 %collective-permute-start.40 = (bf16[512,128]{1,0:T(8,128)(2,1)}, bf16[512,128]{1,0:T(8,128)(2,1)S(1)}, u32[]{:S(2)}, u32[]{:S(2)}) collective-permute-start(bf16[512,128]{1,0:T(8,128)(2,1)} %pad_maximum_fusion.70), channel_id=1, source_target_pairs={{0,8},{8,0},{1,9},{9,1},{2,10},{10,2},{3,11},{11,3},{4,12},{12,4},... | collective-permute-start | bytes 393224 | tf_op jit(solution)/shard_map/ppermute | solution.py:77
  579.8 24.7 %collective-permute-start.53 = (bf16[2048,512]{1,0:T(8,128)(2,1)S(1)}, bf16[2048,512]{1,0:T(8,128)(2,1)S(1)}, u32[]{:S(2)}, u32[]{:S(2)}) collective-permute-start(bf16[2048,512]{1,0:T(8,128)(2,1)S(1)} %copy-done.2), channel_id=1, source_target_pairs={{0,16},{16,0},{1,17},{17,1},{2,18},{18,2},{3,19},{19,3},{4,20},{20... | collective-permute-start | bytes 6291464 | tf_op jit(solution)/shard_map/ppermute | solution.py:77
  579.8 24.7 %collective-permute-start.54 = (bf16[2048,512]{1,0:T(8,128)(2,1)S(1)}, bf16[2048,512]{1,0:T(8,128)(2,1)S(1)}, u32[]{:S(2)}, u32[]{:S(2)}) collective-permute-start(bf16[2048,512]{1,0:T(8,128)(2,1)S(1)} %copy-done.93), channel_id=1, source_target_pairs={{0,16},{16,0},{1,17},{17,1},{2,18},{18,2},{3,19},{19,3},{4,20},{20... | collective-permute-start | bytes 6291464 | tf_op jit(solution)/shard_map/ppermute | solution.py:77
  604.5 28.2 %collective-permute-start.42 = (bf16[2048,512]{1,0:T(8,128)(2,1)S(1)}, bf16[2048,512]{1,0:T(8,128)(2,1)}, u32[]{:S(2)}, u32[]{:S(2)}) collective-permute-start(bf16[2048,512]{1,0:T(8,128)(2,1)S(1)} %copy-done), channel_id=1, source_target_pairs={{0,16},{16,0},{1,17},{17,1},{2,18},{18,2},{3,19},{19,3},{4,20},{20... | collective-permute-start | bytes 6291464 | tf_op jit(solution)/shard_map/ppermute | solution.py:77
  680.9 22.5 %collective-permute-start.67 = (bf16[2048,512]{1,0:T(8,128)(2,1)S(1)}, bf16[2048,512]{1,0:T(8,128)(2,1)S(1)}, u32[]{:S(2)}, u32[]{:S(2)}) collective-permute-start(bf16[2048,512]{1,0:T(8,128)(2,1)S(1)} %convolution_convert_fusion.9), channel_id=1, source_target_pairs={{0,16},{16,0},{1,17},{17,1},{2,18},{18,2},{3,19},{19,3},{4,20},{20... | collective-permute-start | bytes 6291464 | tf_op jit(solution)/shard_map/ppermute | solution.py:77
  707.0 177.2 %reduce-scatter.11.cloned.1.call-start = ((), (), s32[]{:S(2)}) async-start(), calls=%async_computation.29 | async-start | bytes 3145728 | tf_op jit(solution)/shard_map/reduce_scatter | solution.py:433
  711.4 40.9 %collective-permute-start.73 = (bf16[2048,512]{1,0:T(8,128)(2,1)}, bf16[2048,512]{1,0:T(8,128)(2,1)}, u32[]{:S(2)}, u32[]{:S(2)}) collective-permute-start(bf16[2048,512]{1,0:T(8,128)(2,1)} %convolution_convert_fusion.8), channel_id=1, source_target_pairs={{0,16},{16,0},{1,17},{17,1},{2,18},{18,2},{3,19},{19,3},{4,20},{20... | collective-permute-start | bytes 6291464 | tf_op jit(solution)/shard_map/ppermute | solution.py:77
  756.8 127.5 %reduce-scatter.13.cloned.1.call-start = ((), (), s32[]{:S(2)}) async-start(), calls=%async_computation.30 | async-start | bytes 3145728 | tf_op jit(solution)/shard_map/reduce_scatter | solution.py:433
  757.6 230.0 %reduce-scatter.15.cloned.1.call-start = ((), (), s32[]{:S(2)}) async-start(), calls=%async_computation.31 | async-start | bytes 2359296 | tf_op jit(solution)/shard_map/reduce_scatter | solution.py:433
  770.5 33.3 %collective-permute-start.74 = (bf16[512,128]{1,0:T(8,128)(2,1)S(1)}, bf16[512,128]{1,0:T(8,128)(2,1)S(1)}, u32[]{:S(2)}, u32[]{:S(2)}) collective-permute-start(bf16[512,128]{1,0:T(8,128)(2,1)S(1)} %fusion.160), channel_id=1, source_target_pairs={{0,8},{8,0},{1,9},{9,1},{2,10},{10,2},{3,11},{11,3},{4,12},{12,4},... | collective-permute-start | bytes 393224 | tf_op jit(solution)/shard_map/ppermute | solution.py:77
  814.0 31.0 %collective-permute-start.80 = (bf16[2048,384]{0,1:T(8,128)(2,1)S(1)}, bf16[2048,384]{0,1:T(8,128)(2,1)S(1)}, u32[]{:S(2)}, u32[]{:S(2)}) collective-permute-start(bf16[2048,384]{0,1:T(8,128)(2,1)S(1)} %pad_maximum_fusion.1), channel_id=1, source_target_pairs={{0,16},{16,0},{1,17},{17,1},{2,18},{18,2},{3,19},{19,3},{4,20},{20... | collective-permute-start | bytes 4718600 | tf_op jit(solution)/shard_map/ppermute | solution.py:77
  888.5 21.5 %collective-permute-start.86 = (bf16[2048,512]{1,0:T(8,128)(2,1)}, bf16[2048,512]{1,0:T(8,128)(2,1)}, u32[]{:S(2)}, u32[]{:S(2)}) collective-permute-start(bf16[2048,512]{1,0:T(8,128)(2,1)} %convolution_convert_fusion.6), channel_id=1, source_target_pairs={{0,16},{16,0},{1,17},{17,1},{2,18},{18,2},{3,19},{19,3},{4,20},{20... | collective-permute-start | bytes 6291464 | tf_op jit(solution)/shard_map/ppermute | solution.py:77
  888.5 50.1 %all-to-all-start.4 = ((bf16[4,256,512]{2,1,0:T(8,128)(2,1)}), bf16[4,256,512]{2,1,0:T(8,128)(2,1)S(1)}, u32[]{:S(2)}, u32[]{:S(2)}) async-start(bf16[4,256,512]{2,1,0:T(8,128)(2,1)} %bitcast.277), calls=%async_computation.8 | async-start | bytes 2097152 | tf_op jit(solution)/shard_map/all_to_all | solution.py:72
  893.1 147.2 %reduce-scatter.17.cloned.1.call-start = ((), (), s32[]{:S(2)}) async-start(), calls=%async_computation.32 | async-start | bytes 3145728 | tf_op jit(solution)/shard_map/reduce_scatter | solution.py:433
  924.2 58.8 %collective-permute-start.92 = (bf16[2048,512]{1,0:T(8,128)(2,1)}, bf16[2048,512]{1,0:T(8,128)(2,1)}, u32[]{:S(2)}, u32[]{:S(2)}) collective-permute-start(bf16[2048,512]{1,0:T(8,128)(2,1)} %convolution_convert_fusion.5), channel_id=1, source_target_pairs={{0,16},{16,0},{1,17},{17,1},{2,18},{18,2},{3,19},{19,3},{4,20},{20... | collective-permute-start | bytes 6291464 | tf_op jit(solution)/shard_map/ppermute | solution.py:77
  938.7 48.9 %all-to-all-start.5 = ((bf16[4,256,512]{2,1,0:T(8,128)(2,1)}), bf16[4,256,512]{2,1,0:T(8,128)(2,1)}, u32[]{:S(2)}, u32[]{:S(2)}) async-start(bf16[4,256,512]{2,1,0:T(8,128)(2,1)} %bitcast.275), calls=%async_computation.9 | async-start | bytes 2097152 | tf_op jit(solution)/shard_map/all_to_all | solution.py:72
  943.1 122.3 %reduce-scatter.19.cloned.1.call-start = ((), (), s32[]{:S(2)}) async-start(), calls=%async_computation.33 | async-start | bytes 3145728 | tf_op jit(solution)/shard_map/reduce_scatter | solution.py:433
  944.5 38.5 %collective-permute-start.91 = (bf16[64,2048]{1,0:T(8,128)(2,1)S(1)}, bf16[64,2048]{1,0:T(8,128)(2,1)S(1)}, u32[]{:S(2)}, u32[]{:S(2)}) collective-permute-start(bf16[64,2048]{1,0:T(8,128)(2,1)S(1)} %fusion.53), channel_id=1, source_target_pairs={{0,4},{1,5},{2,6},{3,7},{4,0},{5,1},{6,2},{7,3},{8,12},{9,13},{10,... | collective-permute-start | bytes 786440 | tf_op jit(solution)/shard_map/ppermute | solution.py:77
  992.8 36.9 %collective-permute-start.98 = (bf16[2048,512]{1,0:T(8,128)(2,1)}, bf16[2048,512]{1,0:T(8,128)(2,1)}, u32[]{:S(2)}, u32[]{:S(2)}) collective-permute-start(bf16[2048,512]{1,0:T(8,128)(2,1)} %convolution_convert_fusion.4), channel_id=1, source_target_pairs={{0,16},{16,0},{1,17},{17,1},{2,18},{18,2},{3,19},{19,3},{4,20},{20... | collective-permute-start | bytes 6291464 | tf_op jit(solution)/shard_map/ppermute | solution.py:77
  998.4 36.4 %all-to-all-start.6 = ((bf16[4,256,512]{2,1,0:T(8,128)(2,1)}), bf16[4,256,512]{2,1,0:T(8,128)(2,1)S(1)}, u32[]{:S(2)}, u32[]{:S(2)}) async-start(bf16[4,256,512]{2,1,0:T(8,128)(2,1)} %bitcast.274), calls=%async_computation.11 | async-start | bytes 2097152 | tf_op jit(solution)/shard_map/all_to_all | solution.py:72
  1003.1 15.3 %collective-permute-start.95 = (bf16[256,1024]{1,0:T(8,128)(2,1)S(1)}, bf16[256,1024]{1,0:T(8,128)(2,1)}, u32[]{:S(2)}, u32[]{:S(2)}) collective-permute-start(bf16[256,1024]{1,0:T(8,128)(2,1)S(1)} %pad_maximum_fusion.45.left_ref), channel_id=1, source_target_pairs={{0,1},{1,0},{2,3},{3,2},{4,5},{5,4},{6,7},{7,6},{8,9},{9,8},{10,11... | collective-permute-start | bytes 1572872 | tf_op jit(solution)/shard_map/ppermute | solution.py:77
  1010.4 15.4 %collective-permute-start.97 = (bf16[256,1024]{1,0:T(8,128)(2,1)S(1)}, bf16[256,1024]{1,0:T(8,128)(2,1)}, u32[]{:S(2)}, u32[]{:S(2)}) collective-permute-start(bf16[256,1024]{1,0:T(8,128)(2,1)S(1)} %pad_maximum_fusion.46.right_ref), channel_id=1, source_target_pairs={{0,2},{1,3},{2,0},{3,1},{4,6},{5,7},{6,4},{7,5},{8,10},{9,11},{10,... | collective-permute-start | bytes 1572872 | tf_op jit(solution)/shard_map/ppermute | solution.py:77
  1035.8 29.5 %all-to-all-start.7 = ((bf16[4,256,384]{2,1,0:T(8,128)(2,1)}), bf16[4,256,384]{2,1,0:T(8,128)(2,1)}, u32[]{:S(2)}, u32[]{:S(2)}) async-start(bf16[4,256,384]{2,1,0:T(8,128)(2,1)} %bitcast.84), calls=%async_computation.13 | async-start | bytes 1572864 | tf_op jit(solution)/shard_map/all_to_all | solution.py:72
  1040.1 90.1 %reduce-scatter.21.cloned.1.call-start = ((), (), s32[]{:S(2)}) async-start(), calls=%async_computation.34 | async-start | bytes 3145728 | tf_op jit(solution)/shard_map/reduce_scatter | solution.py:433
  1070.8 23.3 %collective-permute-start.100 = (bf16[256,1024]{1,0:T(8,128)(2,1)}, bf16[256,1024]{1,0:T(8,128)(2,1)}, u32[]{:S(2)}, u32[]{:S(2)}) collective-permute-start(bf16[256,1024]{1,0:T(8,128)(2,1)} %slice.1025), channel_id=1, source_target_pairs={{0,1},{1,0},{2,3},{3,2},{4,5},{5,4},{6,7},{7,6},{8,9},{9,8},{10,11... | collective-permute-start | bytes 1572872 | tf_op jit(solution)/shard_map/ppermute | solution.py:77
  1073.0 20.1 %collective-permute-start.102 = (bf16[256,1024]{1,0:T(8,128)(2,1)}, bf16[256,1024]{1,0:T(8,128)(2,1)S(1)}, u32[]{:S(2)}, u32[]{:S(2)}) collective-permute-start(bf16[256,1024]{1,0:T(8,128)(2,1)} %pad_maximum_fusion.48), channel_id=1, source_target_pairs={{0,2},{1,3},{2,0},{3,1},{4,6},{5,7},{6,4},{7,5},{8,10},{9,11},{10,... | collective-permute-start | bytes 1572872 | tf_op jit(solution)/shard_map/ppermute | solution.py:77
  1075.2 29.9 %all-to-all-start.9 = ((bf16[4,256,512]{2,1,0:T(8,128)(2,1)}), bf16[4,256,512]{2,1,0:T(8,128)(2,1)}, u32[]{:S(2)}, u32[]{:S(2)}) async-start(bf16[4,256,512]{2,1,0:T(8,128)(2,1)} %bitcast.278), calls=%async_computation.17 | async-start | bytes 2097152 | tf_op jit(solution)/shard_map/all_to_all | solution.py:72
  1081.8 43.6 %collective-permute-start.105 = (bf16[2048,384]{0,1:T(8,128)(2,1)}, bf16[2048,384]{0,1:T(8,128)(2,1)}, u32[]{:S(2)}, u32[]{:S(2)}) collective-permute-start(bf16[2048,384]{0,1:T(8,128)(2,1)} %pad_maximum_fusion.2), channel_id=1, source_target_pairs={{0,16},{16,0},{1,17},{17,1},{2,18},{18,2},{3,19},{19,3},{4,20},{20... | collective-permute-start | bytes 4718600 | tf_op jit(solution)/shard_map/ppermute | solution.py:77
  1103.0 18.3 %collective-permute-start.104 = (bf16[64,2048]{1,0:T(8,128)(2,1)}, bf16[64,2048]{1,0:T(8,128)(2,1)}, u32[]{:S(2)}, u32[]{:S(2)}) collective-permute-start(bf16[64,2048]{1,0:T(8,128)(2,1)} %fusion.50), channel_id=1, source_target_pairs={{0,4},{1,5},{2,6},{3,7},{4,0},{5,1},{6,2},{7,3},{8,12},{9,13},{10,... | collective-permute-start | bytes 786440 | tf_op jit(solution)/shard_map/ppermute | solution.py:77
  1105.1 25.0 %all-to-all-start.8 = ((bf16[4,256,512]{2,1,0:T(8,128)(2,1)}), bf16[4,256,512]{2,1,0:T(8,128)(2,1)}, u32[]{:S(2)}, u32[]{:S(2)}) async-start(bf16[4,256,512]{2,1,0:T(8,128)(2,1)} %bitcast.276), calls=%async_computation.15 | async-start | bytes 2097152 | tf_op jit(solution)/shard_map/all_to_all | solution.py:72
  1109.4 74.8 %reduce-scatter.23.cloned.1.call-start = ((), (), s32[]{:S(2)}) async-start(), calls=%async_computation.35 | async-start | bytes 2359296 | tf_op jit(solution)/shard_map/reduce_scatter | solution.py:433
  1125.3 38.2 %collective-permute-start.113 = (bf16[4,256,512]{2,1,0:T(8,128)(2,1)}, bf16[4,256,512]{2,1,0:T(8,128)(2,1)}, u32[]{:S(2)}, u32[]{:S(2)}) collective-permute-start(bf16[4,256,512]{2,1,0:T(8,128)(2,1)} %get-tuple-element.348), channel_id=1, source_target_pairs={{0,16},{16,0},{1,17},{17,1},{2,18},{18,2},{3,19},{19,3},{4,20},{20... | collective-permute-start | bytes 3145736 | tf_op jit(solution)/shard_map/ppermute | solution.py:77
  1130.4 26.2 %all-to-all-start.10 = ((bf16[4,256,512]{2,1,0:T(8,128)(2,1)}), bf16[4,256,512]{2,1,0:T(8,128)(2,1)}, u32[]{:S(2)}, u32[]{:S(2)}) async-start(bf16[4,256,512]{2,1,0:T(8,128)(2,1)} %bitcast.279), calls=%async_computation.18 | async-start | bytes 2097152 | tf_op jit(solution)/shard_map/all_to_all | solution.py:72
  1137.5 32.4 %collective-permute-start.112 = (bf16[4,256,512]{2,1,0:T(8,128)(2,1)}, bf16[4,256,512]{2,1,0:T(8,128)(2,1)S(1)}, u32[]{:S(2)}, u32[]{:S(2)}) collective-permute-start(bf16[4,256,512]{2,1,0:T(8,128)(2,1)} %get-tuple-element.350), channel_id=1, source_target_pairs={{0,16},{16,0},{1,17},{17,1},{2,18},{18,2},{3,19},{19,3},{4,20},{20... | collective-permute-start | bytes 3145736 | tf_op jit(solution)/shard_map/ppermute | solution.py:77
  1138.1 21.6 %collective-permute-start.108 = (f32[2,1024]{1,0:T(2,128)S(1)}, f32[2,1024]{1,0:T(2,128)S(1)}, u32[]{:S(2)}, u32[]{:S(2)}) collective-permute-start(f32[2,1024]{1,0:T(2,128)S(1)} %slice_bitcast_fusion), channel_id=1, source_target_pairs={{0,8},{8,0},{1,9},{9,1},{2,10},{10,2},{3,11},{11,3},{4,12},{12,4},... | collective-permute-start | bytes 24584 | tf_op jit(solution)/shard_map/ppermute | solution.py:77
  1159.7 18.0 %collective-permute-start.114 = (bf16[4,256,512]{2,1,0:T(8,128)(2,1)}, bf16[4,256,512]{2,1,0:T(8,128)(2,1)}, u32[]{:S(2)}, u32[]{:S(2)}) collective-permute-start(bf16[4,256,512]{2,1,0:T(8,128)(2,1)} %get-tuple-element.346), channel_id=1, source_target_pairs={{0,16},{16,0},{1,17},{17,1},{2,18},{18,2},{3,19},{19,3},{4,20},{20... | collective-permute-start | bytes 3145736 | tf_op jit(solution)/shard_map/ppermute | solution.py:77
  1159.7 30.3 %collective-permute-start.109 = (f32[2,512]{1,0:T(2,128)S(1)}, f32[2,512]{1,0:T(2,128)S(1)}, u32[]{:S(2)}, u32[]{:S(2)}) collective-permute-start(f32[2,512]{1,0:T(2,128)S(1)} %broadcast_select_fusion.14), channel_id=1, source_target_pairs={{0,4},{1,5},{2,6},{3,7},{4,0},{5,1},{6,2},{7,3},{8,12},{9,13},{10,... | collective-permute-start | bytes 12296 | tf_op jit(solution)/shard_map/ppermute | solution.py:77
  1186.5 16.4 %all-to-all-start.11 = ((bf16[4,256,384]{2,1,0:T(8,128)(2,1)}), bf16[4,256,384]{2,1,0:T(8,128)(2,1)S(1)}, u32[]{:S(2)}, u32[]{:S(2)}) async-start(bf16[4,256,384]{2,1,0:T(8,128)(2,1)} %bitcast.105), calls=%async_computation.19 | async-start | bytes 1572864 | tf_op jit(solution)/shard_map/all_to_all | solution.py:72
  (245 other events, 3264.4 us)
Sparse Core Ops, SparseCore 0:
  55.1 44.2 all-gather.8
  120.9 47.1 all-gather.10
  175.9 56.0 all-gather.12
  259.6 54.8 all-gather.14
  323.2 54.7 all-gather.16
  380.0 55.6 all-gather.18
  437.8 55.5 all-gather.20
  494.9 59.7 all-gather.22
  707.2 55.1 reduce-scatter.8
  764.6 59.4 reduce-scatter.10
  826.3 52.9 reduce-scatter.12
  881.5 42.8 reduce-scatter.14
  926.7 54.2 reduce-scatter.16
  993.0 56.8 reduce-scatter.18
  1064.3 54.6 reduce-scatter.20
  1130.5 44.2 reduce-scatter.22
